TPU v7x, 512 devices: a whole 4x8x8 slice. The times are simulated.
512 devices in a mesh: ctx: 64 (over z, x, core), dp: 8 (over y).
Axes of the slice: x: 4, y: 8, z: 8, core: 2. Of those that a mesh axis runs over, the one named last changes fastest.
Arguments:
- tokens: bfloat16 [8, 8192, 5376], P('dp', 'ctx'), may hold values from -6 to 6
- norm_gain: bfloat16 [5376], replicated, may hold values from 0.5 to 1.5
- queries: bfloat16 [8, 8192, 128], P('dp', 'ctx'), may hold values from -6 to 6
- values: bfloat16 [8, 8192, 128], P('dp', 'ctx'), may hold values from -6 to 6
- upstream: bfloat16 [8, 8192, 128], P('dp', 'ctx'), may hold values from -6 to 6
- segments: int32 [8, 8192], P('dp', 'ctx'), may hold values from 0 to 7, never falling along the last dimension, each value on 1 to 2048 neighbouring positions
- key_weight: bfloat16 [5376, 128], P('ctx', 'dp'), may hold values from -0.078125 to 0.078125
- key_gain: float32 [128], replicated, may hold values from 0.25 to 1.75
- direction: float32 [5376, 128], P('ctx', 'dp'), may hold values from -6 to 6
- stored_basis: float32 [6, 5376, 128], P(None, 'ctx', 'dp'), may hold values from -103.68593 to 103.68593
Outputs:
- coefficients: float32 [7], replicated
- beta: float32 [], replicated
- next_vector: float32 [5376, 128], P('ctx', 'dp')
Inputs may be any that keep to these rules, and one draw needn't show every extreme that they name: `segments`: within each sequence the document ids never fall; each document holds 1 to 2048 tokens, and one of them exactly that many.
All inputs are finite; a program needn't handle non-finite values.
Results may differ from a plain program's by a relative error of at most 0.0035.
The roundings to bfloat16 on the way count: a program that leaves them out, or rounds other values in their place, can miss the bound.
Values may be sent and summed in bfloat16 or wider, within the bound.
A program may use at most 64 MiB of HBM per device.

v0:
```python
import jax
import jax.numpy as jnp
from jax import lax
from jax.sharding import PartitionSpec as P

D = 5376
HD = 128
WINDOW = 1024


SCORE_SCALE = 168.0 ** (-0.5)
EPSILON = 1e-06


def from_behind(value, axis, steps):
    count = lax.axis_size(axis)
    initial, last = (max(0, -steps), min(count, count - steps))
    return lax.ppermute(value, axis, [(source, source + steps) for source in range(initial, last)])


def normalize(activations, gain_vector):
    floats = activations.astype(jnp.float32)
    scaled = floats * lax.rsqrt(jnp.mean(floats * floats, axis=-1, keepdims=True) + EPSILON)
    return (scaled * gain_vector.astype(jnp.float32)).astype(jnp.bfloat16)


def rotate(vectors, places):
    half_width = vectors.shape[-1] // 2
    freqs = 10000.0 ** (-jnp.arange(half_width, dtype=jnp.float32) / half_width)
    angles = places.astype(jnp.float32)[:, None] * freqs[None, :]
    cosine = jnp.cos(angles)
    sine = jnp.sin(angles)
    first_half = vectors[:, :half_width]
    second_half = vectors[:, half_width:]
    return jnp.concatenate(
        [first_half * cosine - second_half * sine, second_half * cosine + first_half * sine], axis=1
    )


def key_map(linear, places, scales):
    normed_keys = (
        linear * lax.rsqrt(jnp.mean(linear * linear, axis=-1, keepdims=True) + EPSILON) * scales
    )
    return rotate(normed_keys, places)


def key_cotangent(linear, cotangent, places, scales):
    return jax.vjp(lambda inner: key_map(inner, places, scales), linear)[1](cotangent)[0]


def band_mask(query_pos, query_doc, key_pos, key_doc):
    near = (key_pos[None, :] <= query_pos[:, None]) & (
        key_pos[None, :] > query_pos[:, None] - WINDOW
    )
    return near & (key_pos[None, :] >= 0) & (key_doc[None, :] == query_doc[:, None])


def band_loss(key_cat, query_rows, value_cat, upstream_rows, allowed):
    scores = jnp.dot(query_rows, key_cat.T, precision=lax.Precision.HIGHEST) * SCORE_SCALE
    expos = jnp.where(allowed, jnp.exp(scores), 0.0)
    weights = expos / jnp.sum(expos, axis=-1, keepdims=True)
    output = jnp.dot(weights, value_cat, precision=lax.Precision.HIGHEST)
    return jnp.sum(upstream_rows * output)


def band_grads(key_cat, key_tan, query_rows, value_cat, upstream_rows, allowed):

    def gradient(keys_in):
        return jax.grad(band_loss)(keys_in, query_rows, value_cat, upstream_rows, allowed)

    return jax.jvp(gradient, (key_cat,), (key_tan,))


def body(
    tokens,
    norm_gain,
    queries,
    values,
    upstream,
    segments,
    key_weight,
    key_gain,
    direction,
    stored_basis,
):
    tok_rows = tokens.shape[1]
    reach = (WINDOW + tok_rows - 1) // tok_rows
    normed = normalize(tokens[0], norm_gain)
    tangent = (direction * D ** (-0.5)).astype(jnp.bfloat16)
    columns = (
        lax.all_gather(key_weight, "dp", axis=1, tiled=True),
        lax.all_gather(tangent, "dp", axis=1, tiled=True),
    )
    block = normed
    key_lin = jnp.dot(
        block,
        lax.all_gather(columns[0], "ctx", axis=0, tiled=True),
        preferred_element_type=jnp.float32,
    )
    tangent_lin = jnp.dot(
        block,
        lax.all_gather(columns[1], "ctx", axis=0, tiled=True),
        preferred_element_type=jnp.float32,
    )
    first_place = lax.axis_index("ctx") * tok_rows
    places = first_place + jnp.arange(tok_rows, dtype=jnp.int32)
    keyed, keyed_tan = jax.jvp(
        lambda inner: key_map(inner, places, key_gain), (key_lin,), (tangent_lin,)
    )
    value_rows = values[0].astype(jnp.float32)
    doc_rows = segments[0].astype(jnp.float32)
    earlier = [
        from_behind((keyed, keyed_tan, value_rows, doc_rows), "ctx", offset)
        for offset in range(1, reach + 1)
    ]
    ordered = earlier[::-1] + [(keyed, keyed_tan, value_rows, doc_rows)]
    key_cat = jnp.concatenate([member[0] for member in ordered], axis=0)
    tan_cat = jnp.concatenate([member[1] for member in ordered], axis=0)
    value_cat = jnp.concatenate([member[2] for member in ordered], axis=0)
    doc_cat = jnp.concatenate([member[3] for member in ordered], axis=0)
    key_pos = first_place - reach * tok_rows + jnp.arange((reach + 1) * tok_rows, dtype=jnp.int32)
    allowed = band_mask(places, doc_rows, key_pos, doc_cat)
    grads, grads_tan = band_grads(
        key_cat,
        tan_cat,
        queries[0].astype(jnp.float32),
        value_cat,
        upstream[0].astype(jnp.float32),
        allowed,
    )
    outgoing = [
        (
            grads[(reach - offset) * tok_rows : (reach - offset + 1) * tok_rows],
            grads_tan[(reach - offset) * tok_rows : (reach - offset + 1) * tok_rows],
        )
        for offset in range(1, reach + 1)
    ]
    grad_keys = grads[reach * tok_rows :]
    grad_tan = grads_tan[reach * tok_rows :]
    for offset in range(1, reach + 1):
        arrived = from_behind((outgoing[offset - 1][0], outgoing[offset - 1][1]), "ctx", -offset)
        grad_keys = grad_keys + arrived[0]
        grad_tan = grad_tan + arrived[1]
    _, cot_tan = jax.jvp(
        lambda inner, cotangent: key_cotangent(inner, cotangent, places, key_gain),
        (key_lin, grad_keys),
        (tangent_lin, grad_tan),
    )
    rounded = cot_tan.astype(jnp.bfloat16)
    block = normed
    row_sums = lax.psum_scatter(
        lax.dot_general(
            block, rounded, (((0,), (0,)), ((), ())), preferred_element_type=jnp.float32
        ),
        "ctx",
        scatter_dimension=0,
        tiled=True,
    )
    product = lax.psum_scatter(row_sums, "dp", scatter_dimension=1, tiled=True) * D ** (-0.5)
    stacked = jnp.concatenate([stored_basis, direction[None]], axis=0)
    entries = D * HD
    local_proj = jnp.einsum("kdh,dh->k", stacked, product, precision=lax.Precision.HIGHEST)
    coefficients = lax.psum(local_proj, ("ctx", "dp")) / entries
    residual = product - jnp.einsum(
        "k,kdh->dh", coefficients, stacked, precision=lax.Precision.HIGHEST
    )
    squared = lax.psum(jnp.sum(residual * residual), ("ctx", "dp")) / entries
    beta = jnp.sqrt(squared + EPSILON)
    return (coefficients, beta, residual / beta)


def solution(mesh):
    in_specs = (
        P("dp", "ctx", None),
        P(),
        P("dp", "ctx", None),
        P("dp", "ctx", None),
        P("dp", "ctx", None),
        P("dp", "ctx"),
        P("ctx", "dp"),
        P(),
        P("ctx", "dp"),
        P(None, "ctx", "dp"),
    )
    out_specs = (P(), P(), P("ctx", "dp"))
    return jax.shard_map(body, mesh=mesh, in_specs=in_specs, out_specs=out_specs, check_vma=False)
```

profile of v0, /device:TPU:1, one launch (start us, length us, event | category | flops | bytes accessed | tf_op | source)
XLA Modules:
  0.0 662.3 jit_solution(9781685123189182002)
XLA Ops:
  8.0 20.5 %all_gather.12 = bf16[84,128]{0,1:T(8,128)(2,1)S(1)} all-gather(bf16[84,16]{0,1:T(8,128)(2,1)S(1)} %multiply_convert_fusion), channel_id=1, replica_groups=mesh['ctx'=64,'dp'=8] {'dp'}, dimensions={1}, use_global_device_ids=true | all-gather | bytes 24192 | tf_op jit(solution)/shard_map/all_gather | solution.py:92
  29.9 4.0 collective-permute-start
  33.9 11.2 %collective-permute-start.1 = (f32[128]{0:T(128)S(1)}, f32[128]{0:T(128)S(1)}, u32[]{:S(2)}, u32[]{:S(2)}) collective-permute-start(f32[128]{0:T(128)S(1)} %convert_bitcast_fusion), channel_id=1, source_target_pairs={{0,56},{8,64},{16,72},{24,80},{32,88},{40,96},{48,104},{56,112},{6... | collective-permute-start | bytes 1544 | tf_op jit(solution)/shard_map/ppermute | solution.py:18
  45.1 4.4 collective-permute-start.2
  49.5 2.5 collective-permute-start.3
  52.0 3.9 collective-permute-start.4
  55.9 19.0 %all_gather.14 = bf16[84,128]{0,1:T(8,128)(2,1)S(1)} all-gather(bf16[84,16]{0,1:T(8,128)(2,1)} %param.16), channel_id=1, replica_groups=mesh['ctx'=64,'dp'=8] {'dp'}, dimensions={1}, use_global_device_ids=true | all-gather | bytes 24192 | tf_op jit(solution)/shard_map/all_gather | solution.py:91
  77.5 13.8 %collective-permute-start.5 = (f32[128]{0:T(128)S(1)}, f32[128]{0:T(128)S(1)}, u32[]{:S(2)}, u32[]{:S(2)}) collective-permute-start(f32[128]{0:T(128)S(1)} %convert_bitcast_fusion), channel_id=1, source_target_pairs={{0,24},{8,32},{16,40},{24,48},{32,56},{40,64},{48,72},{56,80},{64,... | collective-permute-start | bytes 1544 | tf_op jit(solution)/shard_map/ppermute | solution.py:18
  91.4 2.5 collective-permute-start.6
  95.9 3.1 collective-permute-start.24
  99.0 3.8 collective-permute-start.25
  102.8 4.9 collective-permute-start.26
  107.7 3.0 collective-permute-start.27
  110.8 3.4 collective-permute-start.28
  114.3 3.5 collective-permute-start.29
  117.8 2.1 collective-permute-start.30
  119.9 3.4 collective-permute-start.31
  124.6 2.3 reshape.130
  127.8 78.1 %all-gather.7.cloned.1.call-done = bf16[64,84,128]{2,1,0:T(8,128)(2,1)} async-done(((bf16[1,84,128]{2,1,0:T(8,128)(2,1)}), bf16[64,84,128]{2,1,0:T(8,128)(2,1)}) %all-gather.7.cloned.1.call-update) | async-done | bytes 1376272 | tf_op jit(solution)/shard_map/all_gather | solution.py:97
  205.9 2.2 reshape.132
  209.3 2.3 collective-permute-start.8
  211.7 3.8 collective-permute-start.9
  215.5 2.5 collective-permute-start.10
  218.0 4.6 collective-permute-start.11
  222.6 4.2 collective-permute-start.12
  226.7 3.1 collective-permute-start.13
  229.9 2.4 collective-permute-start.14
  232.4 3.0 collective-permute-start.15
  235.4 3.0 collective-permute-start.16
  240.1 4.7 collective-permute-start.18
  244.8 3.9 collective-permute-start.19
  248.7 2.5 collective-permute-start.20
  251.3 4.0 collective-permute-start.21
  256.8 3.4 collective-permute-start.23
  280.1 2.7 collective-permute-start.40
  297.3 2.9 collective-permute-done.45
  300.1 3.3 collective-permute-done.46
  306.5 84.7 %fusion = f32[96,128]{1,0:T(8,128)S(1)} fusion(f32[5376,128]{1,0:T(8,128)S(1)} %fusion.75), kind=kCustom, calls=%all-reduce-scatter | all-reduce-scatter fusion | flops 786433 | bytes 2803712
  391.3 3.7 collective-permute-start.48
  395.0 2.7 collective-permute-start.49
  397.8 3.2 collective-permute-start.55
  400.9 3.4 collective-permute-start.50
  404.3 2.3 collective-permute-start.51
  406.7 5.2 collective-permute-start.52
  413.6 5.1 collective-permute-start.54
  422.9 30.6 %reduce-scatter.6.cloned.1.call-done = f32[16,84]{1,0:T(8,128)} async-done(((f32[128,84]{1,0:T(8,128)}), f32[16,84]{1,0:T(8,128)}) %reduce-scatter.6.cloned.1.call-update) | async-done | bytes 5392
  454.4 103.1 %psum.14 = f32[7]{0:T(128)S(1)} all-reduce(f32[7]{0:T(128)S(1)} %convolution_bitcast_fusion), channel_id=1, replica_groups=mesh['ctx'=64,'dp'=8] {'ctx','dp'}, use_global_device_ids=true, to_apply=%region_11.12 | all-reduce | flops 7 | bytes 56 | tf_op jit(solution)/shard_map/psum | solution.py:163
  559.1 93.5 %psum.15 = f32[]{:T(128)} all-reduce(f32[]{:T(128)} %multiply_reduce_fusion.3), channel_id=1, replica_groups=mesh['ctx'=64,'dp'=8] {'ctx','dp'}, use_global_device_ids=true, to_apply=%region_13.14 | all-reduce | flops 1 | bytes 8 | tf_op jit(solution)/shard_map/psum | solution.py:167
  (187 shorter events, 59.1 us)
Async XLA Ops:
  7.2 117.4 %all-gather.5.cloned.1.call-start = ((), (), s32[]{:S(2)}) async-start(), calls=%async_computation.1 | async-start | bytes 1464320 | tf_op jit(solution)/shard_map/all_gather | solution.py:102
  29.2 176.8 %all-gather.7.cloned.1.call-start = ((), (), s32[]{:S(2)}) async-start(), calls=%async_computation.2 | async-start | bytes 1464320 | tf_op jit(solution)/shard_map/all_gather | solution.py:97
  29.9 47.6 %collective-permute-start = (f32[128]{0:T(128)S(1)}, f32[128]{0:T(128)S(1)}, u32[]{:S(2)}, u32[]{:S(2)}) collective-permute-start(f32[128]{0:T(128)S(1)} %convert_bitcast_fusion), channel_id=1, source_target_pairs={{0,64},{8,72},{16,80},{24,88},{32,96},{40,104},{48,112},{56,120},{... | collective-permute-start | bytes 1544 | tf_op jit(solution)/shard_map/ppermute | solution.py:18
  33.9 57.5 %collective-permute-start.1 = (f32[128]{0:T(128)S(1)}, f32[128]{0:T(128)S(1)}, u32[]{:S(2)}, u32[]{:S(2)}) collective-permute-start(f32[128]{0:T(128)S(1)} %convert_bitcast_fusion), channel_id=1, source_target_pairs={{0,56},{8,64},{16,72},{24,80},{32,88},{40,96},{48,104},{56,112},{6... | collective-permute-start | bytes 1544 | tf_op jit(solution)/shard_map/ppermute | solution.py:18
  45.1 48.8 %collective-permute-start.2 = (f32[128]{0:T(128)S(1)}, f32[128]{0:T(128)S(1)}, u32[]{:S(2)}, u32[]{:S(2)}) collective-permute-start(f32[128]{0:T(128)S(1)} %convert_bitcast_fusion), channel_id=1, source_target_pairs={{0,48},{8,56},{16,64},{24,72},{32,80},{40,88},{48,96},{56,104},{64... | collective-permute-start | bytes 1544 | tf_op jit(solution)/shard_map/ppermute | solution.py:18
  49.5 46.4 %collective-permute-start.3 = (f32[128]{0:T(128)S(1)}, f32[128]{0:T(128)S(1)}, u32[]{:S(2)}, u32[]{:S(2)}) collective-permute-start(f32[128]{0:T(128)S(1)} %convert_bitcast_fusion), channel_id=1, source_target_pairs={{0,40},{8,48},{16,56},{24,64},{32,72},{40,80},{48,88},{56,96},{64,... | collective-permute-start | bytes 1544 | tf_op jit(solution)/shard_map/ppermute | solution.py:18
  52.0 47.0 %collective-permute-start.4 = (f32[128]{0:T(128)S(1)}, f32[128]{0:T(128)S(1)}, u32[]{:S(2)}, u32[]{:S(2)}) collective-permute-start(f32[128]{0:T(128)S(1)} %convert_bitcast_fusion), channel_id=1, source_target_pairs={{0,32},{8,40},{16,48},{24,56},{32,64},{40,72},{48,80},{56,88},{64,... | collective-permute-start | bytes 1544 | tf_op jit(solution)/shard_map/ppermute | solution.py:18
  75.6 377.9 %reduce-scatter.6.cloned.1.call-start = ((), (), s32[]{:S(2)}) async-start(), calls=%async_computation.3 | async-start | bytes 73728
  77.5 25.3 %collective-permute-start.5 = (f32[128]{0:T(128)S(1)}, f32[128]{0:T(128)S(1)}, u32[]{:S(2)}, u32[]{:S(2)}) collective-permute-start(f32[128]{0:T(128)S(1)} %convert_bitcast_fusion), channel_id=1, source_target_pairs={{0,24},{8,32},{16,40},{24,48},{32,56},{40,64},{48,72},{56,80},{64,... | collective-permute-start | bytes 1544 | tf_op jit(solution)/shard_map/ppermute | solution.py:18
  91.4 16.3 %collective-permute-start.6 = (f32[128]{0:T(128)S(1)}, f32[128]{0:T(128)S(1)}, u32[]{:S(2)}, u32[]{:S(2)}) collective-permute-start(f32[128]{0:T(128)S(1)} %convert_bitcast_fusion), channel_id=1, source_target_pairs={{0,16},{8,24},{16,32},{24,40},{32,48},{40,56},{48,64},{56,72},{64,... | collective-permute-start | bytes 1544 | tf_op jit(solution)/shard_map/ppermute | solution.py:18
  93.9 16.9 %collective-permute-start.7 = (f32[128]{0:T(128)S(1)}, f32[128]{0:T(128)S(1)}, u32[]{:S(2)}, u32[]{:S(2)}) collective-permute-start(f32[128]{0:T(128)S(1)} %convert_bitcast_fusion), channel_id=1, source_target_pairs={{0,8},{8,16},{16,24},{24,32},{32,40},{40,48},{48,56},{56,64},{64,7... | collective-permute-start | bytes 1544 | tf_op jit(solution)/shard_map/ppermute | solution.py:18
  95.9 18.4 %collective-permute-start.24 = (f32[128,128]{1,0:T(8,128)S(1)}, f32[128,128]{1,0:T(8,128)S(1)}, u32[]{:S(2)}, u32[]{:S(2)}) collective-permute-start(f32[128,128]{1,0:T(8,128)S(1)} %bitcast_convert_fusion), channel_id=1, source_target_pairs={{0,64},{8,72},{16,80},{24,88},{32,96},{40,104},{48,112},{56,120},{... | collective-permute-start | bytes 196616 | tf_op jit(solution)/shard_map/ppermute | solution.py:18
  99.0 18.8 %collective-permute-start.25 = (f32[128,128]{1,0:T(8,128)S(1)}, f32[128,128]{1,0:T(8,128)S(1)}, u32[]{:S(2)}, u32[]{:S(2)}) collective-permute-start(f32[128,128]{1,0:T(8,128)S(1)} %bitcast_convert_fusion), channel_id=1, source_target_pairs={{0,56},{8,64},{16,72},{24,80},{32,88},{40,96},{48,104},{56,112},{6... | collective-permute-start | bytes 196616 | tf_op jit(solution)/shard_map/ppermute | solution.py:18
  102.8 17.1 %collective-permute-start.26 = (f32[128,128]{1,0:T(8,128)S(1)}, f32[128,128]{1,0:T(8,128)S(1)}, u32[]{:S(2)}, u32[]{:S(2)}) collective-permute-start(f32[128,128]{1,0:T(8,128)S(1)} %bitcast_convert_fusion), channel_id=1, source_target_pairs={{0,48},{8,56},{16,64},{24,72},{32,80},{40,88},{48,96},{56,104},{64... | collective-permute-start | bytes 196616 | tf_op jit(solution)/shard_map/ppermute | solution.py:18
  107.7 15.6 %collective-permute-start.27 = (f32[128,128]{1,0:T(8,128)S(1)}, f32[128,128]{1,0:T(8,128)S(1)}, u32[]{:S(2)}, u32[]{:S(2)}) collective-permute-start(f32[128,128]{1,0:T(8,128)S(1)} %bitcast_convert_fusion), channel_id=1, source_target_pairs={{0,40},{8,48},{16,56},{24,64},{32,72},{40,80},{48,88},{56,96},{64,... | collective-permute-start | bytes 196616 | tf_op jit(solution)/shard_map/ppermute | solution.py:18
  110.8 12.5 %collective-permute-start.28 = (f32[128,128]{1,0:T(8,128)S(1)}, f32[128,128]{1,0:T(8,128)S(1)}, u32[]{:S(2)}, u32[]{:S(2)}) collective-permute-start(f32[128,128]{1,0:T(8,128)S(1)} %bitcast_convert_fusion), channel_id=1, source_target_pairs={{0,32},{8,40},{16,48},{24,56},{32,64},{40,72},{48,80},{56,88},{64,... | collective-permute-start | bytes 196616 | tf_op jit(solution)/shard_map/ppermute | solution.py:18
  114.3 9.1 %collective-permute-start.29 = (f32[128,128]{1,0:T(8,128)S(1)}, f32[128,128]{1,0:T(8,128)S(1)}, u32[]{:S(2)}, u32[]{:S(2)}) collective-permute-start(f32[128,128]{1,0:T(8,128)S(1)} %bitcast_convert_fusion), channel_id=1, source_target_pairs={{0,24},{8,32},{16,40},{24,48},{32,56},{40,64},{48,72},{56,80},{64,... | collective-permute-start | bytes 196616 | tf_op jit(solution)/shard_map/ppermute | solution.py:18
  209.3 17.4 %collective-permute-start.8 = (f32[128,128]{0,1:T(8,128)S(1)}, f32[128,128]{0,1:T(8,128)S(1)}, u32[]{:S(2)}, u32[]{:S(2)}) collective-permute-start(f32[128,128]{0,1:T(8,128)S(1)} %pad_maximum_fusion), channel_id=1, source_target_pairs={{0,64},{8,72},{16,80},{24,88},{32,96},{40,104},{48,112},{56,120},{... | collective-permute-start | bytes 196616 | tf_op jit(solution)/shard_map/ppermute | solution.py:18
  211.7 18.2 %collective-permute-start.9 = (f32[128,128]{0,1:T(8,128)S(1)}, f32[128,128]{0,1:T(8,128)S(1)}, u32[]{:S(2)}, u32[]{:S(2)}) collective-permute-start(f32[128,128]{0,1:T(8,128)S(1)} %pad_maximum_fusion), channel_id=1, source_target_pairs={{0,56},{8,64},{16,72},{24,80},{32,88},{40,96},{48,104},{56,112},{6... | collective-permute-start | bytes 196616 | tf_op jit(solution)/shard_map/ppermute | solution.py:18
  215.5 16.9 %collective-permute-start.10 = (f32[128,128]{0,1:T(8,128)S(1)}, f32[128,128]{0,1:T(8,128)S(1)}, u32[]{:S(2)}, u32[]{:S(2)}) collective-permute-start(f32[128,128]{0,1:T(8,128)S(1)} %pad_maximum_fusion), channel_id=1, source_target_pairs={{0,48},{8,56},{16,64},{24,72},{32,80},{40,88},{48,96},{56,104},{64... | collective-permute-start | bytes 196616 | tf_op jit(solution)/shard_map/ppermute | solution.py:18
  218.0 17.4 %collective-permute-start.11 = (f32[128,128]{0,1:T(8,128)S(1)}, f32[128,128]{0,1:T(8,128)S(1)}, u32[]{:S(2)}, u32[]{:S(2)}) collective-permute-start(f32[128,128]{0,1:T(8,128)S(1)} %pad_maximum_fusion), channel_id=1, source_target_pairs={{0,40},{8,48},{16,56},{24,64},{32,72},{40,80},{48,88},{56,96},{64,... | collective-permute-start | bytes 196616 | tf_op jit(solution)/shard_map/ppermute | solution.py:18
  222.6 15.9 %collective-permute-start.12 = (f32[128,128]{0,1:T(8,128)S(1)}, f32[128,128]{0,1:T(8,128)S(1)}, u32[]{:S(2)}, u32[]{:S(2)}) collective-permute-start(f32[128,128]{0,1:T(8,128)S(1)} %pad_maximum_fusion), channel_id=1, source_target_pairs={{0,32},{8,40},{16,48},{24,56},{32,64},{40,72},{48,80},{56,88},{64,... | collective-permute-start | bytes 196616 | tf_op jit(solution)/shard_map/ppermute | solution.py:18
  226.7 13.3 %collective-permute-start.13 = (f32[128,128]{0,1:T(8,128)S(1)}, f32[128,128]{0,1:T(8,128)S(1)}, u32[]{:S(2)}, u32[]{:S(2)}) collective-permute-start(f32[128,128]{0,1:T(8,128)S(1)} %pad_maximum_fusion), channel_id=1, source_target_pairs={{0,24},{8,32},{16,40},{24,48},{32,56},{40,64},{48,72},{56,80},{64,... | collective-permute-start | bytes 196616 | tf_op jit(solution)/shard_map/ppermute | solution.py:18
  229.9 14.9 %collective-permute-start.14 = (f32[128,128]{0,1:T(8,128)S(1)}, f32[128,128]{0,1:T(8,128)S(1)}, u32[]{:S(2)}, u32[]{:S(2)}) collective-permute-start(f32[128,128]{0,1:T(8,128)S(1)} %pad_maximum_fusion), channel_id=1, source_target_pairs={{0,16},{8,24},{16,32},{24,40},{32,48},{40,56},{48,64},{56,72},{64,... | collective-permute-start | bytes 196616 | tf_op jit(solution)/shard_map/ppermute | solution.py:18
  232.4 16.3 %collective-permute-start.15 = (f32[128,128]{0,1:T(8,128)S(1)}, f32[128,128]{0,1:T(8,128)S(1)}, u32[]{:S(2)}, u32[]{:S(2)}) collective-permute-start(f32[128,128]{0,1:T(8,128)S(1)} %pad_maximum_fusion), channel_id=1, source_target_pairs={{0,8},{8,16},{16,24},{24,32},{32,40},{40,48},{48,56},{56,64},{64,7... | collective-permute-start | bytes 196616 | tf_op jit(solution)/shard_map/ppermute | solution.py:18
  235.4 15.9 %collective-permute-start.16 = (f32[128,128]{0,1:T(8,128)S(1)}, f32[128,128]{0,1:T(8,128)S(1)}, u32[]{:S(2)}, u32[]{:S(2)}) collective-permute-start(f32[128,128]{0,1:T(8,128)S(1)} %pad_maximum_fusion.1), channel_id=1, source_target_pairs={{0,64},{8,72},{16,80},{24,88},{32,96},{40,104},{48,112},{56,120},{... | collective-permute-start | bytes 196616 | tf_op jit(solution)/shard_map/ppermute | solution.py:18
  238.4 16.9 %collective-permute-start.17 = (f32[128,128]{0,1:T(8,128)S(1)}, f32[128,128]{0,1:T(8,128)S(1)}, u32[]{:S(2)}, u32[]{:S(2)}) collective-permute-start(f32[128,128]{0,1:T(8,128)S(1)} %pad_maximum_fusion.1), channel_id=1, source_target_pairs={{0,56},{8,64},{16,72},{24,80},{32,88},{40,96},{48,104},{56,112},{6... | collective-permute-start | bytes 196616 | tf_op jit(solution)/shard_map/ppermute | solution.py:18
  240.1 16.7 %collective-permute-start.18 = (f32[128,128]{0,1:T(8,128)S(1)}, f32[128,128]{0,1:T(8,128)S(1)}, u32[]{:S(2)}, u32[]{:S(2)}) collective-permute-start(f32[128,128]{0,1:T(8,128)S(1)} %pad_maximum_fusion.1), channel_id=1, source_target_pairs={{0,48},{8,56},{16,64},{24,72},{32,80},{40,88},{48,96},{56,104},{64... | collective-permute-start | bytes 196616 | tf_op jit(solution)/shard_map/ppermute | solution.py:18
  244.8 15.3 %collective-permute-start.19 = (f32[128,128]{0,1:T(8,128)S(1)}, f32[128,128]{0,1:T(8,128)S(1)}, u32[]{:S(2)}, u32[]{:S(2)}) collective-permute-start(f32[128,128]{0,1:T(8,128)S(1)} %pad_maximum_fusion.1), channel_id=1, source_target_pairs={{0,40},{8,48},{16,56},{24,64},{32,72},{40,80},{48,88},{56,96},{64,... | collective-permute-start | bytes 196616 | tf_op jit(solution)/shard_map/ppermute | solution.py:18
  248.7 11.5 %collective-permute-start.20 = (f32[128,128]{0,1:T(8,128)S(1)}, f32[128,128]{0,1:T(8,128)S(1)}, u32[]{:S(2)}, u32[]{:S(2)}) collective-permute-start(f32[128,128]{0,1:T(8,128)S(1)} %pad_maximum_fusion.1), channel_id=1, source_target_pairs={{0,32},{8,40},{16,48},{24,56},{32,64},{40,72},{48,80},{56,88},{64,... | collective-permute-start | bytes 196616 | tf_op jit(solution)/shard_map/ppermute | solution.py:18
  251.3 8.9 %collective-permute-start.21 = (f32[128,128]{0,1:T(8,128)S(1)}, f32[128,128]{0,1:T(8,128)S(1)}, u32[]{:S(2)}, u32[]{:S(2)}) collective-permute-start(f32[128,128]{0,1:T(8,128)S(1)} %pad_maximum_fusion.1), channel_id=1, source_target_pairs={{0,24},{8,32},{16,40},{24,48},{32,56},{40,64},{48,72},{56,80},{64,... | collective-permute-start | bytes 196616 | tf_op jit(solution)/shard_map/ppermute | solution.py:18
  269.1 8.9 %collective-permute-start.34 = (f32[128,128]{0,1:T(8,128)S(1)}, f32[128,128]{0,1:T(8,128)S(1)}, u32[]{:S(2)}, u32[]{:S(2)}) collective-permute-start(f32[128,128]{0,1:T(8,128)S(1)} %get-tuple-element.33), channel_id=1, source_target_pairs={{24,0},{32,8},{40,16},{48,24},{56,32},{64,40},{72,48},{80,56},{88,... | collective-permute-start | bytes 196616 | tf_op jit(solution)/shard_map/ppermute | solution.py:18
  270.4 9.6 %collective-permute-start.35 = (f32[128,128]{0,1:T(8,128)S(1)}, f32[128,128]{0,1:T(8,128)S(1)}, u32[]{:S(2)}, u32[]{:S(2)}) collective-permute-start(f32[128,128]{0,1:T(8,128)S(1)} %get-tuple-element.32), channel_id=1, source_target_pairs={{32,0},{40,8},{48,16},{56,24},{64,32},{72,40},{80,48},{88,56},{96,... | collective-permute-start | bytes 196616 | tf_op jit(solution)/shard_map/ppermute | solution.py:18
  271.7 11.1 %collective-permute-start.36 = (f32[128,128]{0,1:T(8,128)S(1)}, f32[128,128]{0,1:T(8,128)S(1)}, u32[]{:S(2)}, u32[]{:S(2)}) collective-permute-start(f32[128,128]{0,1:T(8,128)S(1)} %get-tuple-element.31), channel_id=1, source_target_pairs={{40,0},{48,8},{56,16},{64,24},{72,32},{80,40},{88,48},{96,56},{104... | collective-permute-start | bytes 196616 | tf_op jit(solution)/shard_map/ppermute | solution.py:18
  273.1 11.5 %collective-permute-start.37 = (f32[128,128]{0,1:T(8,128)S(1)}, f32[128,128]{0,1:T(8,128)S(1)}, u32[]{:S(2)}, u32[]{:S(2)}) collective-permute-start(f32[128,128]{0,1:T(8,128)S(1)} %get-tuple-element.30), channel_id=1, source_target_pairs={{48,0},{56,8},{64,16},{72,24},{80,32},{88,40},{96,48},{104,56},{11... | collective-permute-start | bytes 196616 | tf_op jit(solution)/shard_map/ppermute | solution.py:18
  274.7 13.2 %collective-permute-start.38 = (f32[128,128]{0,1:T(8,128)S(1)}, f32[128,128]{0,1:T(8,128)S(1)}, u32[]{:S(2)}, u32[]{:S(2)}) collective-permute-start(f32[128,128]{0,1:T(8,128)S(1)} %get-tuple-element.29), channel_id=1, source_target_pairs={{56,0},{64,8},{72,16},{80,24},{88,32},{96,40},{104,48},{112,56},{1... | collective-permute-start | bytes 196616 | tf_op jit(solution)/shard_map/ppermute | solution.py:18
  278.0 11.2 %collective-permute-start.39 = (f32[128,128]{0,1:T(8,128)S(1)}, f32[128,128]{0,1:T(8,128)S(1)}, u32[]{:S(2)}, u32[]{:S(2)}) collective-permute-start(f32[128,128]{0,1:T(8,128)S(1)} %get-tuple-element.28), channel_id=1, source_target_pairs={{64,0},{72,8},{80,16},{88,24},{96,32},{104,40},{112,48},{120,56},{... | collective-permute-start | bytes 196616 | tf_op jit(solution)/shard_map/ppermute | solution.py:18
  280.1 10.5 %collective-permute-start.40 = (f32[128,128]{0,1:T(8,128)S(1)}, f32[128,128]{0,1:T(8,128)S(1)}, u32[]{:S(2)}, u32[]{:S(2)}) collective-permute-start(f32[128,128]{0,1:T(8,128)S(1)} %get-tuple-element.19), channel_id=1, source_target_pairs={{8,0},{16,8},{24,16},{32,24},{40,32},{48,40},{56,48},{64,56},{72,6... | collective-permute-start | bytes 196616 | tf_op jit(solution)/shard_map/ppermute | solution.py:18
  282.8 9.1 %collective-permute-start.41 = (f32[128,128]{0,1:T(8,128)S(1)}, f32[128,128]{0,1:T(8,128)S(1)}, u32[]{:S(2)}, u32[]{:S(2)}) collective-permute-start(f32[128,128]{0,1:T(8,128)S(1)} %get-tuple-element.26), channel_id=1, source_target_pairs={{16,0},{24,8},{32,16},{40,24},{48,32},{56,40},{64,48},{72,56},{80,... | collective-permute-start | bytes 196616 | tf_op jit(solution)/shard_map/ppermute | solution.py:18
  290.6 9.6 %collective-permute-start.45 = (f32[128,128]{0,1:T(8,128)S(1)}, f32[128,128]{0,1:T(8,128)S(1)}, u32[]{:S(2)}, u32[]{:S(2)}) collective-permute-start(f32[128,128]{0,1:T(8,128)S(1)} %get-tuple-element.22), channel_id=1, source_target_pairs={{48,0},{56,8},{64,16},{72,24},{80,32},{88,40},{96,48},{104,56},{11... | collective-permute-start | bytes 196616 | tf_op jit(solution)/shard_map/ppermute | solution.py:18
  291.9 11.6 %collective-permute-start.46 = (f32[128,128]{0,1:T(8,128)S(1)}, f32[128,128]{0,1:T(8,128)S(1)}, u32[]{:S(2)}, u32[]{:S(2)}) collective-permute-start(f32[128,128]{0,1:T(8,128)S(1)} %get-tuple-element.21), channel_id=1, source_target_pairs={{56,0},{64,8},{72,16},{80,24},{88,32},{96,40},{104,48},{112,56},{1... | collective-permute-start | bytes 196616 | tf_op jit(solution)/shard_map/ppermute | solution.py:18
  293.2 12.3 %collective-permute-start.47 = (f32[128,128]{0,1:T(8,128)S(1)}, f32[128,128]{0,1:T(8,128)S(1)}, u32[]{:S(2)}, u32[]{:S(2)}) collective-permute-start(f32[128,128]{0,1:T(8,128)S(1)} %get-tuple-element.20), channel_id=1, source_target_pairs={{64,0},{72,8},{80,16},{88,24},{96,32},{104,40},{112,48},{120,56},{... | collective-permute-start | bytes 196616 | tf_op jit(solution)/shard_map/ppermute | solution.py:18
  391.3 20.6 %collective-permute-start.48 = (f32[96,128]{1,0:T(8,128)S(1)}, f32[96,128]{1,0:T(8,128)S(1)}, u32[]{:S(2)}, u32[]{:S(2)}) collective-permute-start(f32[96,128]{1,0:T(8,128)S(1)} %fusion), channel_id=1, source_target_pairs={{0,8},{8,16},{16,24},{24,32},{32,40},{40,48},{48,56},{56,64},{64,7... | collective-permute-start | bytes 147464
  395.0 18.5 %collective-permute-start.49 = (f32[96,128]{1,0:T(8,128)S(1)}, f32[96,128]{1,0:T(8,128)S(1)}, u32[]{:S(2)}, u32[]{:S(2)}) collective-permute-start(f32[96,128]{1,0:T(8,128)S(1)} %fusion), channel_id=1, source_target_pairs={{0,16},{8,24},{16,32},{24,40},{32,48},{40,56},{48,64},{56,72},{64,... | collective-permute-start | bytes 147464
  397.8 8.9 %collective-permute-start.55 = (f32[84,128]{1,0:T(8,128)S(1)}, f32[84,128]{1,0:T(8,128)S(1)}, u32[]{:S(2)}, u32[]{:S(2)}) collective-permute-start(f32[84,128]{1,0:T(8,128)S(1)} %slice.110), channel_id=1, source_target_pairs={{0,64},{8,72},{16,80},{24,88},{32,96},{40,104},{48,112},{56,120},{... | collective-permute-start | bytes 129032
  400.9 19.7 %collective-permute-start.50 = (f32[96,128]{1,0:T(8,128)S(1)}, f32[96,128]{1,0:T(8,128)S(1)}, u32[]{:S(2)}, u32[]{:S(2)}) collective-permute-start(f32[96,128]{1,0:T(8,128)S(1)} %fusion), channel_id=1, source_target_pairs={{0,24},{8,32},{16,40},{24,48},{32,56},{40,64},{48,72},{56,80},{64,... | collective-permute-start | bytes 147464
  404.3 16.3 %collective-permute-start.51 = (f32[96,128]{1,0:T(8,128)S(1)}, f32[96,128]{1,0:T(8,128)S(1)}, u32[]{:S(2)}, u32[]{:S(2)}) collective-permute-start(f32[96,128]{1,0:T(8,128)S(1)} %fusion), channel_id=1, source_target_pairs={{0,32},{8,40},{16,48},{24,56},{32,64},{40,72},{48,80},{56,88},{64,... | collective-permute-start | bytes 147464
  406.7 13.9 %collective-permute-start.52 = (f32[96,128]{1,0:T(8,128)S(1)}, f32[96,128]{1,0:T(8,128)S(1)}, u32[]{:S(2)}, u32[]{:S(2)}) collective-permute-start(f32[96,128]{1,0:T(8,128)S(1)} %fusion), channel_id=1, source_target_pairs={{0,40},{8,48},{16,56},{24,64},{32,72},{40,80},{48,88},{56,96},{64,... | collective-permute-start | bytes 147464
  (22 other events, 944.1 us)
Sparse Core Ops, SparseCore 0:
  29.3 92.8 all-gather.4
  125.5 80.3 all-gather.6
  423.0 30.5 reduce-scatter.5
where the time goes:
time: 665 us; the launch traced here: 662 us
  blocking collectives  321 us (48%)
  starting transfers between devices  172 us (26%)
  waiting for transfers between devices  128 us (19%)
  between operations  17.7 us (3%)
  local copies, waits for them, and re-layouts  9.79 us (1%)
  other arithmetic  7.2 us (1%)
  matrix products  6.96 us (1%)
    ppermute x48, starting transfers between devices, from_behind(): lax.ppermute(value, axis, [(source, source + steps) for source in range(i...  145 us
    psum x1, blocking collectives, body(): coefficients = lax.psum(local_proj, ('ctx', 'dp')) / entries  103 us
    psum x1, blocking collectives, body(): squared = lax.psum(jnp.sum(residual * residual), ('ctx', 'dp')) / entries  93.5 us
    unnamed x1, blocking collectives  84.7 us
    all_gather x1, waiting for transfers between devices, body(): lax.all_gather(columns[0], 'ctx', axis=0, tiled=True)  78.1 us
    unnamed x12, waiting for transfers between devices  30.7 us
    unnamed x9, starting transfers between devices  27.3 us
    all_gather x1, blocking collectives, body(): lax.all_gather(tangent, 'dp', axis=1, tiled=True)  20.5 us
  transfers between devices with their start and end apart: 59, of which 15 were waited for; matrix products, arithmetic and copies ran while one was open for 1% of the time, Pallas kernels for 0%

commit v1 on v0

v1 whole, which is shorter than its diff:
```python
import jax
import jax.numpy as jnp
import numpy as np
from jax import lax
from jax.experimental import pallas as pl
from jax.experimental.pallas import tpu as pltpu
from jax.sharding import PartitionSpec as P

D = 5376
HD = 128
WINDOW = 1024
HALF = D // 2
ROWS = 84
SCORE_SCALE = 168.0 ** (-0.5)
EPSILON = 1e-06
ENTRIES = D * HD
GROUP = 768
LOW = -1e30
MESH = pl.DeviceIdType.MESH
F32 = jnp.float32
BF16 = jnp.bfloat16
FREQS = np.tile(10000.0 ** (-np.arange(64) / 64.0), 2)[None].astype(np.float32)


def dot_nt(a, b):
    return lax.dot_general(a, b, (((1,), (1,)), ((), ())), preferred_element_type=F32)


def dot_nn(a, b):
    return lax.dot_general(a, b, (((1,), (0,)), ((), ())), preferred_element_type=F32)


def split(a):
    high = a.astype(BF16)
    return high, (a - high.astype(F32)).astype(BF16)


def ring_step(t):
    odd = t % 2
    return odd * (8 - (t + 1) // 2) + (1 - odd) * ((t + 2) // 2)


def far_step(t):
    return ring_step(6 - t)


def kernel(
    tok,
    gain,
    q_in,
    v_in,
    u_in,
    seg_in,
    wt,
    kg,
    freq_in,
    bas,
    out,
    aux,
    g1,
    wb,
    nb,
    ns,
    qu,
    segb,
    kl,
    klr,
    ev,
    sv,
    gv,
    rst,
    cott,
    acc,
    tb,
    rx,
    py,
    ry,
    pz,
    rz,
    ar,
    cs,
    g1_s,
    g1_r,
    qu_s,
    qu_r,
    sg_s,
    sg_r,
    y_s,
    y_r,
    x_s,
    x_r,
    one_s,
    one_r,
    st_s,
    st_r,
    rx_s,
    rx_r,
    ry_s,
    ry_r,
    rz_s,
    rz_r,
    ar_s,
    ar_r,
):
    ctx = lax.axis_index("ctx")
    y = lax.axis_index("dp")
    z = ctx // 8
    x = (ctx // 2) % 4
    k = ctx % 2
    half = z // 4
    zz = z % 4

    def at_z(zi, ki):
        return ((zi * 4 + x) * 2 + ki, y)

    def at_x(xi):
        return ((z * 4 + xi) * 2 + k, y)

    def at_y(yi):
        return (ctx, yi)

    def at_ctx(ci):
        return (ci % 64, y)

    other = ((z * 4 + x) * 2 + (1 - k), y)

    def rdma(src, dst, send, recv, device):
        return pltpu.make_async_remote_copy(
            src_ref=src,
            dst_ref=dst,
            send_sem=send,
            recv_sem=recv,
            device_id=device,
            device_id_type=MESH,
        )

    barrier = pltpu.get_barrier_semaphore()

    def greet(device):
        pl.semaphore_signal(barrier, inc=1, device_id=device, device_id_type=MESH)

    for d in range(1, 9):
        greet(at_ctx(ctx + d))
        greet(at_ctx(ctx + 64 - d))
    for dz in range(2, 7):
        greet(at_z((z + dz) % 8, 0))
        greet(at_z((z + dz) % 8, 1))
    for dz in (1, 7):
        greet(at_z((z + dz) % 8, 1 - k))
    for dy in range(1, 8):
        greet(at_y((y + dy) % 8))

    qu[0, 0] = q_in[...]
    qu[0, 1] = u_in[...]
    segb[0] = jnp.broadcast_to(seg_in[...], (8, 128))
    pl.semaphore_wait(barrier, 35)

    own_slot = zz * 2 + k

    def g1_copy(zi, slot):
        return rdma(wt, g1.at[slot], g1_s.at[zi], g1_r.at[slot], at_z(zi, half))

    def g1_send(t, _):
        zi = (z + t) % 8

        @pl.when(jnp.logical_or(zi != z, half != k))
        def _():
            g1_copy(zi, own_slot).start()

        return 0

    lax.fori_loop(0, 8, g1_send, 0)

    @pl.when(half == k)
    def _():
        g1[own_slot] = wt[...]

    def qu_copy(j):
        return rdma(qu.at[0], qu.at[j], qu_s.at[j - 1], qu_r.at[j - 1], at_ctx(ctx + 64 - j))

    def sg_copy(j):
        return rdma(segb.at[0], segb.at[j], sg_s.at[j - 1], sg_r.at[j - 1], at_ctx(ctx + 64 - j))

    def qu_send(j, _):
        qu_copy(j).start()
        sg_copy(j).start()
        return 0

    lax.fori_loop(1, 9, qu_send, 0)

    lane128 = lax.broadcasted_iota(jnp.int32, (1, 128), 1)
    gain_row = gain[...].astype(F32)

    def norm_chunk(r):
        rows = pl.ds(pl.multiple_of(r * 16, 16), 16)
        floats = tok[rows, :].astype(F32)
        scale = lax.rsqrt(jnp.mean(floats * floats, axis=-1, keepdims=True) + EPSILON)
        normed = floats * scale * gain_row
        for hh in range(2):
            for xi in range(4):
                tiles = [jnp.zeros((16, 128), F32) for _ in range(6)]
                for zi in range(4):
                    start = hh * HALF + zi * 672 + xi * 168
                    first = min(start // 128, D // 128 - 3)
                    shift = start - first * 128
                    goal, lead = (168 * zi) // 128, (168 * zi) % 128
                    slab = normed[:, first * 128 : first * 128 + 384]
                    moved = pltpu.roll(slab, (lead - shift) % 384, 1) if lead != shift else slab
                    for m in range(3):
                        low, high = lead - 128 * m, lead + 168 - 128 * m
                        if high <= 0 or low >= 128:
                            continue
                        part = moved[:, 128 * m : 128 * m + 128]
                        if low > 0 or high < 128:
                            inside = jnp.logical_and(lane128 >= low, lane128 < high)
                            part = jnp.where(inside, part, 0.0)
                        tiles[goal + m] = tiles[goal + m] + part
                group = jnp.concatenate(tiles, axis=1).astype(BF16)

                @pl.when(k == hh)
                def _():
                    nb[xi, pl.ds(pl.multiple_of(k * 128 + r * 16, 16), 16), :] = group

                @pl.when(k != hh)
                def _():
                    ns[xi, rows, :] = group

    norm_chunk(7)

    def g1_wait(slot, _):
        zi = half * 0 + k * 4 + slot // 2
        mine = jnp.logical_and(zi == z, slot % 2 == k)

        @pl.when(jnp.logical_not(mine))
        def _():
            g1_copy(z, slot).wait_recv()

        return 0

    lax.fori_loop(0, 8, g1_wait, 0)
    tiles = [jnp.zeros((32, 128), F32) for _ in range(6)]
    for slot in range(8):
        piece = g1[slot].astype(F32).reshape(32, 128)
        goal, lead = (ROWS * slot) // 128, (ROWS * slot) % 128
        moved = pltpu.roll(piece, lead, 1) if lead else piece
        tiles[goal] = tiles[goal] + jnp.where(lane128 >= lead, moved, 0.0)
        if lead + ROWS > 128:
            tiles[goal + 1] = tiles[goal + 1] + jnp.where(lane128 < lead, moved, 0.0)
    block = jnp.concatenate(tiles, axis=1).astype(BF16)
    my_cols = pl.ds(pl.multiple_of(y * 16, 16), 16)
    wb[x, 0, my_cols, :] = block[0:16]
    wb[x, 1, my_cols, :] = block[16:32]

    def piece_at(xi, yi):
        return wb.at[xi, :, pl.ds(pl.multiple_of(yi * 16, 16), 16), :]

    def y_copy(src_y, dst_y, t):
        return rdma(piece_at(x, src_y), piece_at(x, src_y), y_s.at[t], y_r.at[src_y], at_y(dst_y))

    def x_copy(src_x, yi, dst_x, t):
        return rdma(
            piece_at(src_x, yi), piece_at(src_x, yi), x_s.at[t, yi], x_r.at[src_x, yi], at_x(dst_x)
        )

    def y_send(t, _):
        y_copy(y, (y + far_step(t)) % 8, t).start()
        return 0

    lax.fori_loop(0, 7, y_send, 0)

    def x_send(yi):
        for t, dx in enumerate((2, 1, 3)):
            x_copy(x, yi, (x + dx) % 4, t).start()

    x_send(y)

    def y_forward(t, _):
        norm_chunk(t)
        src = (y + ring_step(t)) % 8
        y_copy(src, y, 0).wait_recv()
        x_send(src)
        return 0

    lax.fori_loop(0, 7, y_forward, 0)

    swap = rdma(ns, nb.at[:, pl.ds(pl.multiple_of(k * 128, 128), 128), :], one_s.at[0], one_r.at[0], other)
    swap.start()

    lane = lax.broadcasted_iota(jnp.int32, (128, 128), 1)
    sub = lax.broadcasted_iota(jnp.int32, (128, 128), 0)
    angle = (ctx * 128 + sub).astype(F32) * freq_in[...]
    cs[0] = jnp.cos(angle)
    cs[1] = jnp.sin(angle) * jnp.where(lane < 64, -1.0, 1.0)
    key_doc = jnp.transpose(jnp.broadcast_to(segb[0, 0:1].astype(F32), (128, 128)))

    lane8 = lax.broadcasted_iota(jnp.int32, (8, 128), 1)
    sub8 = lax.broadcasted_iota(jnp.int32, (8, 128), 0)
    gram = jnp.zeros((8, 128), F32)
    for a in range(7):
        for b in range(a, 7):
            dotted = jnp.sum(jnp.sum(bas[a] * bas[b], axis=0, keepdims=True), axis=1, keepdims=True)
            spot = jnp.logical_and(sub8 == a, lane8 == b)
            if a != b:
                spot = jnp.logical_or(spot, jnp.logical_and(sub8 == b, lane8 == a))
            gram = jnp.where(spot, dotted, gram)

    swap.wait_recv()
    for dx in range(4):
        xi = (x + dx) % 4
        if dx:

            def x_wait(yi, _):
                x_copy(xi, yi, x, 0).wait_recv()
                return 0

            lax.fori_loop(0, 8, x_wait, 0)
        part = dot_nt(nb[xi], wb[xi].reshape(256, GROUP))
        if dx:
            kl[...] += part
        else:
            kl[...] = part
    mine = pl.ds(pl.multiple_of(k * 128, 128), 128)
    theirs = pl.ds(pl.multiple_of((1 - k) * 128, 128), 128)
    kl_swap = rdma(kl.at[theirs], klr, one_s.at[1], one_r.at[1], other)
    kl_swap.start()

    def qu_wait(j, _):
        qu_copy(j).wait_recv()
        sg_copy(j).wait_recv()
        return 0

    lax.fori_loop(1, 9, qu_wait, 0)
    kl_swap.wait_recv()
    both = kl[mine, :] + klr[...]
    lin, tan = both[:, 0:128], both[:, 128:256]
    cosine, sine = cs[0], cs[1]
    key_gain = kg[...]

    def rope(vec):
        return vec * cosine + pltpu.roll(vec, 64, 1) * sine

    def rope_back(vec):
        return vec * cosine - pltpu.roll(vec, 64, 1) * sine

    def mean(vec):
        return jnp.mean(vec, axis=-1, keepdims=True)

    inv = lax.rsqrt(mean(lin * lin) + EPSILON)
    inv3 = inv * inv * inv
    inv_tan = -inv3 * mean(lin * tan)
    keyed = rope(lin * inv * key_gain) * SCORE_SCALE
    keyed_tan = rope((tan * inv + lin * inv_tan) * key_gain) * SCORE_SCALE
    k_high, k_low = split(keyed)
    t_high, t_low = split(keyed_tan)
    stacked_keys = jnp.concatenate([k_high, k_low, t_high, t_low], axis=0)
    value_rows = v_in[...]

    def score(j, _):
        raw = dot_nt(stacked_keys, qu[j, 0])
        s = raw[0:128] + raw[128:256]
        st = raw[256:384] + raw[384:512]
        g = dot_nt(value_rows, qu[j, 1])
        gap = 128 * j + lane - sub
        near = jnp.logical_and(gap >= 0, gap < WINDOW)
        same = key_doc == segb[j, 0:1].astype(F32)
        allowed = jnp.logical_and(jnp.logical_and(near, same), ctx + j < 64)
        top = jnp.max(jnp.where(allowed, s, LOW), axis=0, keepdims=True)
        e = jnp.where(allowed, jnp.exp(s - top), 0.0)
        est = e * st
        rows = [top] + [jnp.sum(m, axis=0, keepdims=True) for m in (e, e * g, est, est * g)]
        rst[8, j] = jnp.concatenate(rows + [jnp.zeros((3, 128), F32)], axis=0)
        ev[j] = e
        sv[j] = st
        gv[j] = g
        return 0

    lax.fori_loop(0, 9, score, 0)

    def st_copies():
        copies = []
        for d in range(1, 9):
            n = 9 - d
            copies.append(
                rdma(
                    rst.at[8, pl.ds(d, n)],
                    rst.at[8 + d, pl.ds(0, n)],
                    st_s.at[d - 1],
                    st_r.at[d - 1],
                    at_ctx(ctx + d),
                )
            )
            copies.append(
                rdma(
                    rst.at[8, pl.ds(0, n)],
                    rst.at[8 - d, pl.ds(d, n)],
                    st_s.at[7 + d],
                    st_r.at[7 + d],
                    at_ctx(ctx + 64 - d),
                )
            )
        return copies

    st_list = st_copies()
    for copy in st_list:
        copy.start()
    for copy in st_list:
        copy.wait_recv()

    def gradient(j, _):
        stats = [rst[8 - j + t, j] for t in range(9)]
        peak = stats[0][0:1]
        for stat in stats[1:]:
            peak = jnp.maximum(peak, stat[0:1])
        total = jnp.zeros((8, 128), F32)
        for stat in stats:
            total = total + jnp.exp(stat[0:1] - peak) * stat
        filled = total[1:2] > 0.0
        scale = jnp.where(filled, 1.0 / jnp.where(filled, total[1:2], 1.0), 0.0)
        m = total[2:3] * scale
        a = total[3:4] * scale
        m_tan = total[4:5] * scale - a * m
        p = ev[j] * (jnp.exp(rst[8, j][0:1] - peak) * scale)
        rest = gv[j] - m
        ds = p * rest
        ds_tan = p * ((sv[j] - a) * rest - m_tan)
        high, low = split(jnp.concatenate([ds, ds_tan], axis=0))
        prod = dot_nn(jnp.concatenate([high, low], axis=0), qu[j, 0])
        acc[...] += prod[0:256] + prod[256:512]
        return 0

    acc[...] = jnp.zeros((256, 128), F32)
    lax.fori_loop(0, 9, gradient, 0)

    w = rope_back(acc[0:128] * SCORE_SCALE) * key_gain
    w_tan = rope_back(acc[128:256] * SCORE_SCALE) * key_gain
    xw = mean(lin * w)
    xw_tan = mean(tan * w) + mean(lin * w_tan)
    cot = (
        inv_tan * w
        + inv * w_tan
        - tan * (inv3 * xw)
        - lin * (3.0 * inv * inv * inv_tan * xw + inv3 * xw_tan)
    )
    cott[k] = jnp.transpose(cot).astype(BF16)
    cot_swap = rdma(cott.at[k], cott.at[k], one_s.at[2], one_r.at[2], other)
    cot_swap.start()
    cot_in = rdma(cott.at[1 - k], cott.at[1 - k], one_s.at[2], one_r.at[2], other)
    cot_in.wait_recv()
    cots = jnp.concatenate([cott[0], cott[1]], axis=1)

    def rx_copy(dx, yi):
        cols = pl.ds(pl.multiple_of(yi * 16, 16), 16)
        return rdma(
            tb.at[dx, cols], rx.at[dx - 1, cols], rx_s.at[dx - 1, yi], rx_r.at[dx - 1, yi], at_x((x + dx) % 4)
        )

    for dx in (2, 1, 3):
        tb[dx] = dot_nn(cots, nb[(x + dx) % 4]).astype(BF16)

    def rx_send(t, _):
        yi = (y + 4 + t) % 8
        for dx in (2, 1, 3):
            rx_copy(dx, yi).start()
        return 0

    lax.fori_loop(0, 8, rx_send, 0)
    kl_own = dot_nn(cots, nb[x])
    tb_own = kl_own.astype(F32)
    py[...] = tb_own

    def rx_sum(yi):
        cols = pl.ds(pl.multiple_of(yi * 16, 16), 16)
        total = py[cols, :]
        for dx in (2, 1, 3):
            rx_copy(dx, yi).wait_recv()
            total = total + rx[dx - 1, cols, :].astype(F32)
        return total

    def ry_copy(t, dy):
        yi = (y + dy) % 8
        cols = pl.ds(pl.multiple_of(yi * 16, 16), 16)
        return rdma(tb.at[0, cols], ry.at[dy], ry_s.at[dy - 1], ry_r.at[dy - 1], at_y(yi))

    def y_sum(t, _):
        dy = (4 + t) % 8
        yi = (y + dy) % 8
        total = rx_sum(yi)
        cols = pl.ds(pl.multiple_of(yi * 16, 16), 16)
        tb[0, cols, :] = total.astype(BF16)
        ry_copy(t, dy).start()
        return 0

    lax.fori_loop(0, 4, y_sum, 0)
    lax.fori_loop(5, 8, y_sum, 0)
    total = rx_sum(y)

    def y_add(dy, _):
        ry_copy(0, dy).wait_recv()
        return 0

    lax.fori_loop(1, 8, y_add, 0)
    for dy in range(1, 8):
        total = total + ry[dy].astype(F32)

    def pz_copy(slot, src_z):
        zi = k * 4 + slot // 2
        return rdma(pz.at[slot], rz.at[src_z], rz_s.at[slot], rz_r.at[src_z], at_z(zi, slot % 2))

    for slot in range(8):
        goal, lead = (ROWS * slot) // 128, (ROWS * slot) % 128
        piece = total[:, goal * 128 : goal * 128 + 128]
        if lead:
            piece = pltpu.roll(piece, 128 - lead, 1)
        if lead + ROWS > 128:
            following = pltpu.roll(total[:, goal * 128 + 128 : goal * 128 + 256], 128 - lead, 1)
            piece = jnp.where(lane128 < 128 - lead, piece, following)
        pz[slot] = jnp.where(lane128 < ROWS, piece, 0.0)

    def pz_self(slot):
        return jnp.logical_and(k * 4 + slot // 2 == z, slot % 2 == k)

    def pz_send(t, _):
        slot = (own_slot + 1 + t) % 8

        @pl.when(jnp.logical_not(pz_self(slot)))
        def _():
            pz_copy(slot, z).start()

        @pl.when(pz_self(slot))
        def _():
            rz[z] = pz[slot]

        return 0

    lax.fori_loop(0, 8, pz_send, 0)

    def rz_wait(t, _):
        src = (z + t) % 8

        @pl.when(jnp.logical_or(src != z, half != k))
        def _():
            pz_copy(0, src).wait_recv()

        return 0

    lax.fori_loop(0, 8, rz_wait, 0)
    product = rz[0]
    for src in range(1, 8):
        product = product + rz[src]
    product = product * D ** (-0.5)

    rows = [jnp.sum(bas[a] * product, axis=0, keepdims=True) for a in range(7)]
    rows.append(jnp.sum(product * product, axis=0, keepdims=True))
    sums = jnp.concatenate(rows + [gram], axis=0)

    def all_sum(stage, value, own, device):
        ar[stage, own] = value

        def copy(src, t, target):
            return rdma(
                ar.at[stage, src], ar.at[stage, src], ar_s.at[stage, t], ar_r.at[stage, src], device(target)
            )

        def send(t, _):
            copy(own, t, (own + far_step(t)) % 8).start()
            return 0

        lax.fori_loop(0, 7, send, 0)

        def wait(t, _):
            copy((own + ring_step(t)) % 8, 0, own).wait_recv()
            return 0

        lax.fori_loop(0, 7, wait, 0)
        total = ar[stage, 0]
        for i in range(1, 8):
            total = total + ar[stage, i]

        def drain(t, _):
            copy(own, t, (own + far_step(t)) % 8).wait_send()
            return 0

        lax.fori_loop(0, 7, drain, 0)
        return total

    sums = all_sum(0, sums, x * 2 + k, lambda i: (z * 8 + i, y))
    sums = all_sum(1, sums, z, lambda i: (i * 8 + x * 2 + k, y))
    sums = all_sum(2, sums, y, lambda i: (ctx, i))
    inner = jnp.sum(sums[0:8], axis=1, keepdims=True)
    coef = jnp.broadcast_to(inner / ENTRIES, (8, 128))
    coef_row = jnp.sum(jnp.where(jnp.logical_and(sub8 == lane8, sub8 < 7), coef, 0.0), axis=0, keepdims=True)
    quad = jnp.sum(coef_row * sums[8:16], axis=1, keepdims=True)
    norm = jnp.where(sub8 < 7, coef * (quad - 2.0 * inner), jnp.broadcast_to(inner, (8, 128)))
    squared = jnp.maximum(jnp.sum(norm, axis=0, keepdims=True), 0.0) / ENTRIES
    beta = jnp.sqrt(squared + EPSILON)
    residual = product
    for a in range(7):
        residual = residual - coef[a : a + 1] * bas[a]
    out[...] = residual / beta
    aux[...] = jnp.where(sub8 < 7, coef, jnp.broadcast_to(beta, (8, 128)))

    def g1_drain(t, _):
        zi = (z + t) % 8

        @pl.when(jnp.logical_or(zi != z, half != k))
        def _():
            g1_copy(zi, own_slot).wait_send()

        return 0

    lax.fori_loop(0, 8, g1_drain, 0)

    def qu_drain(j, _):
        qu_copy(j).wait_send()
        sg_copy(j).wait_send()
        return 0

    lax.fori_loop(1, 9, qu_drain, 0)

    def y_drain(t, _):
        y_copy(y, (y + far_step(t)) % 8, t).wait_send()
        ry_copy(0, t + 1).wait_send()
        return 0

    lax.fori_loop(0, 7, y_drain, 0)

    def x_drain(yi, _):
        for t, dx in enumerate((2, 1, 3)):
            x_copy(x, yi, (x + dx) % 4, t).wait_send()
            rx_copy(dx, yi).wait_send()
        return 0

    lax.fori_loop(0, 8, x_drain, 0)
    swap.wait_send()
    kl_swap.wait_send()
    cot_swap.wait_send()
    for copy in st_list:
        copy.wait_send()

    def pz_drain(slot, _):
        @pl.when(jnp.logical_not(pz_self(slot)))
        def _():
            pz_copy(slot, z).wait_send()

        return 0

    lax.fori_loop(0, 8, pz_drain, 0)


def body(
    tokens,
    norm_gain,
    queries,
    values,
    upstream,
    segments,
    key_weight,
    key_gain,
    direction,
    stored_basis,
):
    tangent = (direction * D ** (-0.5)).astype(BF16)
    pad = ((0, 0), (0, 0), (0, 128 - ROWS))
    wt = jnp.pad(jnp.stack([key_weight.T, tangent.T]), pad)
    stacked = jnp.concatenate([stored_basis, direction[None]], axis=0)
    bas = jnp.pad(jnp.swapaxes(stacked, 1, 2), pad)
    dma = pltpu.SemaphoreType.DMA
    vmem = pl.BlockSpec(memory_space=pltpu.VMEM)
    out, aux = pl.pallas_call(
        kernel,
        out_shape=(jax.ShapeDtypeStruct((16, 128), F32), jax.ShapeDtypeStruct((8, 128), F32)),
        in_specs=[vmem] * 10,
        out_specs=(vmem, vmem),
        scratch_shapes=[
            pltpu.VMEM((8, 2, 16, 128), BF16),
            pltpu.VMEM((4, 2, 128, GROUP), BF16),
            pltpu.VMEM((4, 256, GROUP), BF16),
            pltpu.VMEM((4, 128, GROUP), BF16),
            pltpu.VMEM((9, 2, 128, 128), BF16),
            pltpu.VMEM((9, 8, 128), jnp.int32),
            pltpu.VMEM((256, 256), F32),
            pltpu.VMEM((128, 256), F32),
            pltpu.VMEM((9, 128, 128), F32),
            pltpu.VMEM((9, 128, 128), F32),
            pltpu.VMEM((9, 128, 128), F32),
            pltpu.VMEM((17, 9, 8, 128), F32),
            pltpu.VMEM((2, 128, 128), BF16),
            pltpu.VMEM((256, 128), F32),
            pltpu.VMEM((4, 128, GROUP), BF16),
            pltpu.VMEM((3, 128, GROUP), BF16),
            pltpu.VMEM((128, GROUP), F32),
            pltpu.VMEM((8, 16, GROUP), BF16),
            pltpu.VMEM((8, 16, 128), F32),
            pltpu.VMEM((8, 16, 128), F32),
            pltpu.VMEM((3, 8, 16, 128), F32),
            pltpu.VMEM((2, 128, 128), F32),
            dma((8,)),
            dma((8,)),
            dma((8,)),
            dma((8,)),
            dma((8,)),
            dma((8,)),
            dma((7,)),
            dma((8,)),
            dma((3, 8)),
            dma((4, 8)),
            dma((3,)),
            dma((3,)),
            dma((16,)),
            dma((16,)),
            dma((3, 8)),
            dma((3, 8)),
            dma((7,)),
            dma((7,)),
            dma((8,)),
            dma((8,)),
            dma((3, 7)),
            dma((3, 8)),
        ],
        compiler_params=pltpu.CompilerParams(
            collective_id=0, has_side_effects=True, vmem_limit_bytes=56 * 2**20
        ),
        name="lanczos_step",
    )(
        tokens[0],
        norm_gain[None],
        queries[0],
        values[0],
        upstream[0],
        segments,
        wt,
        key_gain[None],
        jnp.asarray(FREQS),
        bas,
    )
    return aux[:7, 0], aux[7, 0], out[:, :ROWS].T


def solution(mesh):
    in_specs = (
        P("dp", "ctx", None),
        P(),
        P("dp", "ctx", None),
        P("dp", "ctx", None),
        P("dp", "ctx", None),
        P("dp", "ctx"),
        P("ctx", "dp"),
        P(),
        P("ctx", "dp"),
        P(None, "ctx", "dp"),
    )
    out_specs = (P(), P(), P("ctx", "dp"))
    return jax.shard_map(body, mesh=mesh, in_specs=in_specs, out_specs=out_specs, check_vma=False)
```

time: 665 us -> 107 us (0.16)
  blocking collectives: 321 us -> 0 us
  starting transfers between devices: 172 us -> 0 us
  waiting for transfers between devices: 128 us -> 0 us
  Pallas kernels: 0 us -> 96.9 us
  between operations: 17.7 us -> 0.64 us
  matrix products: 6.96 us -> 0 us
    psum x2 -> x0, blocking collectives: 197 us -> none  [the longest x1 103 us: body(): coefficients = lax.psum(local_proj, ('ctx', 'dp')) / entries]
    ppermute x48 -> x0, starting transfers between devices: 145 us -> none  [from_behind(): lax.ppermute(value, axis, [(source, source + steps) for source in range(i...]
    pallas_call x0 -> x1, Pallas kernels: none -> 96.9 us  [body(): pl.pallas_call(kernel, out_shape=(jax.ShapeDtypeStruct((16, 128), F32), j...]
    unnamed x1 -> x0, blocking collectives: 84.7 us -> none
    all_gather x2 -> x0, waiting for transfers between devices: 78.2 us -> none  [the longest x1 78.1 us: body(): lax.all_gather(columns[0], 'ctx', axis=0, tiled=True)]
    all_gather x2 -> x0, blocking collectives: 39.5 us -> none  [the longest x1 20.5 us: body(): lax.all_gather(tangent, 'dp', axis=1, tiled=True)]
    unnamed x12 -> x0, waiting for transfers between devices: 30.7 us -> none
    unnamed x9 -> x0, starting transfers between devices: 27.3 us -> none
  transfers between devices with their start and end apart: 59 -> 0, of which waited for: 15 -> 0; matrix products, arithmetic and copies ran while one was open for 1% -> 0% of each run, Pallas kernels for 0% -> 0%
where the time goes in v1:
time: 107 us; the launch traced here: 106 us
  Pallas kernels  96.9 us (91%)
  local copies, waits for them, and re-layouts  5.74 us (5%)
  other arithmetic  2.81 us (3%)
    pallas_call x1, Pallas kernels, body(): pl.pallas_call(kernel, out_shape=(jax.ShapeDtypeStruct((16, 128), F32), j...  96.9 us
    slice x2, local copies, waits for them, and re-layouts, body(): return (aux[:7, 0], aux[7, 0], out[:, :ROWS].T)  2.5 us

profile of v1, /device:TPU:1, one launch (start us, length us, event | category | flops | bytes accessed | tf_op | source)
XLA Modules:
  0.0 106.1 jit_solution(16433992584629290204)
XLA Ops:
  0.6 0.8 maximum_bitcast_fusion
  1.5 0.6 pad.9.bas
  2.1 1.3 %broadcast_in_dim.9.gain = bf16[1,5376]{1,0:T(2,128)(2,1)} reshape(bf16[5376]{0:T(1024)(128)(2,1)} %param.12) | data formatting | bytes 21504 | tf_op jit(solution)/shard_map/broadcast_in_dim | solution.py:726
  3.4 0.7 fusion.3
  4.1 1.3 %fusion.2.wt = bf16[2,16,128]{2,1,0:T(8,128)(2,1)} fusion(bf16[1,16,84]{2,1,0:T(8,128)(2,1)S(1)} %fusion.3, bf16[1,16,84]{2,1,0:T(8,128)(2,1)} %bitcast.23), kind=kLoop, calls=%fused_computation.4 | loop fusion | flops 28672 | bytes 13568 | tf_op jit(solution)/shard_map/stack | solution.py:664
  5.4 96.9 %lanczos_step.1 = (f32[16,128]{1,0:T(8,128)}, f32[8,128]{1,0:T(8,128)}) custom-call(bf16[128,5376]{1,0:T(8,128)(2,1)} %bitcast.18, bf16[1,5376]{1,0:T(2,128)(2,1)} %broadcast_in_dim.9.gain, bf16[128,128]{1,0:T(8,128)(2,1)} %bitcast.20, bf16[128,128]{1,0:T(8,128)(2,1)} %bitcast.21, bf16[128,128]{1,0:T(8,128)(2,1)} %bitcast.22, s32[1,128]{1,0:T(1,128)} %seg_in.1, ...), custom_call_target="tpu_custom_call" | custom-call | tf_op jit(solution)/shard_map/lanczos_step/pallas_call | solution.py:669
  102.3 1.2 %slice.10 = f32[1,1]{1,0:T(1,128)} slice(f32[8,128]{1,0:T(8,128)} %get-tuple-element.5), slice={[7:8], [0:1]} | slice | bytes 8 | tf_op jit(solution)/shard_map/slice | solution.py:736
  103.5 1.3 %slice_reduce_fusion = f32[7]{0:T(128)} fusion(f32[8,128]{1,0:T(8,128)} %get-tuple-element.5), kind=kLoop, calls=%fused_computation.8 | loop fusion | bytes 56 | tf_op jit(solution)/shard_map/slice | solution.py:736
  104.8 1.3 %slice_bitcast_fusion = f32[84,16]{0,1:T(8,128)} fusion(f32[16,128]{1,0:T(8,128)} %get-tuple-element.6), kind=kLoop, calls=%fused_computation.5 | loop fusion | bytes 10752 | tf_op jit(solution)/shard_map/transpose | solution.py:736

commit v2 on v1

--- a/solution.py
+++ b/solution.py
@@ -51,12 +51,16 @@
     v_in,
     u_in,
     seg_in,
-    wt,
+    w_in,
+    dir_in,
     kg,
     freq_in,
+    bas_in,
+    out,
+    coef_out,
+    beta_out,
+    wt,
     bas,
-    out,
-    aux,
     g1,
     wb,
     nb,
@@ -89,6 +93,8 @@
     y_r,
     x_s,
     x_r,
+    f_s,
+    f_r,
     one_s,
     one_r,
     st_s,
@@ -109,6 +115,8 @@
     k = ctx % 2
     half = z // 4
     zz = z % 4
+    parity = z % 2
+    place = ctx % 8
 
     def at_z(zi, ki):
         return ((zi * 4 + x) * 2 + ki, y)
@@ -123,6 +131,7 @@
         return (ci % 64, y)
 
     other = ((z * 4 + x) * 2 + (1 - k), y)
+    drains = []
 
     def rdma(src, dst, send, recv, device):
         return pltpu.make_async_remote_copy(
@@ -153,12 +162,15 @@
     qu[0, 0] = q_in[...]
     qu[0, 1] = u_in[...]
     segb[0] = jnp.broadcast_to(seg_in[...], (8, 128))
+    wt[...] = jnp.zeros((2, 16, 128), BF16)
+    wt[0, :, 0:ROWS] = w_in[...]
+    wt[1, :, 0:ROWS] = (dir_in[...] * D ** (-0.5)).astype(BF16)
     pl.semaphore_wait(barrier, 35)
 
     own_slot = zz * 2 + k
 
     def g1_copy(zi, slot):
-        return rdma(wt, g1.at[slot], g1_s.at[zi], g1_r.at[slot], at_z(zi, half))
+        return rdma(wt.at[zi % 2], g1.at[slot], g1_s.at[zi], g1_r.at[slot], at_z(zi, half))
 
     def g1_send(t, _):
         zi = (z + t) % 8
@@ -171,25 +183,46 @@
 
     lax.fori_loop(0, 8, g1_send, 0)
 
+    def g1_drain(t, _):
+        zi = (z + t) % 8
+
+        @pl.when(jnp.logical_or(zi != z, half != k))
+        def _():
+            g1_copy(zi, own_slot).wait_send()
+
+        return 0
+
+    drains.append(lambda: lax.fori_loop(0, 8, g1_drain, 0))
+
     @pl.when(half == k)
     def _():
-        g1[own_slot] = wt[...]
-
-    def qu_copy(j):
-        return rdma(qu.at[0], qu.at[j], qu_s.at[j - 1], qu_r.at[j - 1], at_ctx(ctx + 64 - j))
-
-    def sg_copy(j):
-        return rdma(segb.at[0], segb.at[j], sg_s.at[j - 1], sg_r.at[j - 1], at_ctx(ctx + 64 - j))
-
-    def qu_send(j, _):
-        qu_copy(j).start()
-        sg_copy(j).start()
-        return 0
-
-    lax.fori_loop(1, 9, qu_send, 0)
+        g1[own_slot] = wt[parity]
+
+    bas[...] = jnp.zeros((7, 16, 128), F32)
+    bas[0:6, :, 0:ROWS] = bas_in[...]
+    bas[6, :, 0:ROWS] = dir_in[...]
+
+    def qu_far():
+        return [
+            rdma(ref.at[0], ref.at[8], sends.at[7], recvs.at[7], at_ctx(ctx + 56))
+            for ref, sends, recvs in ((qu, qu_s, qu_r), (segb, sg_s, sg_r))
+        ]
+
+    def qu_near(j):
+        source = 8 * ((j + 7 - place) // 8)
+        device = at_ctx(ctx + source + 64 - j)
+        return [
+            rdma(ref.at[source], ref.at[j], sends.at[j - 1], recvs.at[j - 1], device)
+            for ref, sends, recvs in ((qu, qu_s, qu_r), (segb, sg_s, sg_r))
+        ]
+
+    for copy in qu_far():
+        copy.start()
+        drains.append(copy.wait_send)
 
     lane128 = lax.broadcasted_iota(jnp.int32, (1, 128), 1)
-    gain_row = gain[...].astype(F32)
+    gain_tiles = gain[...].astype(F32)
+    gain_row = jnp.concatenate([gain_tiles[i : i + 1] for i in range(D // 128)], axis=1)
 
     def norm_chunk(r):
         rows = pl.ds(pl.multiple_of(r * 16, 16), 16)
@@ -238,41 +271,66 @@
         return 0
 
     lax.fori_loop(0, 8, g1_wait, 0)
-    tiles = [jnp.zeros((32, 128), F32) for _ in range(6)]
+    tiles = [jnp.zeros((16, 128), F32) for _ in range(6)]
     for slot in range(8):
-        piece = g1[slot].astype(F32).reshape(32, 128)
+        piece = g1[slot].astype(F32)
         goal, lead = (ROWS * slot) // 128, (ROWS * slot) % 128
         moved = pltpu.roll(piece, lead, 1) if lead else piece
         tiles[goal] = tiles[goal] + jnp.where(lane128 >= lead, moved, 0.0)
         if lead + ROWS > 128:
             tiles[goal + 1] = tiles[goal + 1] + jnp.where(lane128 < lead, moved, 0.0)
-    block = jnp.concatenate(tiles, axis=1).astype(BF16)
-    my_cols = pl.ds(pl.multiple_of(y * 16, 16), 16)
-    wb[x, 0, my_cols, :] = block[0:16]
-    wb[x, 1, my_cols, :] = block[16:32]
-
-    def piece_at(xi, yi):
-        return wb.at[xi, :, pl.ds(pl.multiple_of(yi * 16, 16), 16), :]
+    wb[x, parity, pl.ds(pl.multiple_of(y * 16, 16), 16), :] = jnp.concatenate(tiles, axis=1).astype(BF16)
+
+    def piece_at(matrix, xi, yi):
+        return wb.at[xi, matrix, pl.ds(pl.multiple_of(yi * 16, 16), 16), :]
 
     def y_copy(src_y, dst_y, t):
-        return rdma(piece_at(x, src_y), piece_at(x, src_y), y_s.at[t], y_r.at[src_y], at_y(dst_y))
+        piece = piece_at(parity, x, src_y)
+        return rdma(piece, piece, y_s.at[t], y_r.at[src_y], at_y(dst_y))
 
     def x_copy(src_x, yi, dst_x, t):
-        return rdma(
-            piece_at(src_x, yi), piece_at(src_x, yi), x_s.at[t, yi], x_r.at[src_x, yi], at_x(dst_x)
-        )
+        piece = piece_at(parity, src_x, yi)
+        return rdma(piece, piece, x_s.at[t, yi], x_r.at[src_x, yi], at_x(dst_x))
+
+    def f_copy(matrix, xi, yi):
+        piece = piece_at(matrix, xi, yi)
+        target = at_z((z + 1 + 6 * (yi % 2)) % 8, k)
+        return rdma(piece, piece, f_s.at[xi, yi], f_r.at[xi, yi], target)
 
     def y_send(t, _):
         y_copy(y, (y + far_step(t)) % 8, t).start()
         return 0
 
     lax.fori_loop(0, 7, y_send, 0)
+
+    def y_drain(t, _):
+        y_copy(y, (y + far_step(t)) % 8, t).wait_send()
+        return 0
+
+    drains.append(lambda: lax.fori_loop(0, 7, y_drain, 0))
 
     def x_send(yi):
         for t, dx in enumerate((2, 1, 3)):
             x_copy(x, yi, (x + dx) % 4, t).start()
+        f_copy(parity, x, yi).start()
 
     x_send(y)
+    for copy in qu_far():
+        copy.wait_recv()
+
+    def qu_send(j, _):
+        for copy in qu_near(j):
+            copy.start()
+        return 0
+
+    lax.fori_loop(1, 8, qu_send, 0)
+
+    def qu_drain(j, _):
+        for copy in qu_near(j):
+            copy.wait_send()
+        return 0
+
+    drains.append(lambda: lax.fori_loop(1, 8, qu_drain, 0))
 
     def y_forward(t, _):
         norm_chunk(t)
@@ -283,8 +341,30 @@
 
     lax.fori_loop(0, 7, y_forward, 0)
 
-    swap = rdma(ns, nb.at[:, pl.ds(pl.multiple_of(k * 128, 128), 128), :], one_s.at[0], one_r.at[0], other)
+    def x_drain(yi, _):
+        for t, dx in enumerate((2, 1, 3)):
+            x_copy(x, yi, (x + dx) % 4, t).wait_send()
+        for xi in range(4):
+            f_copy(parity, xi, yi).wait_send()
+        return 0
+
+    drains.append(lambda: lax.fori_loop(0, 8, x_drain, 0))
+
+    swap = rdma(
+        ns, nb.at[:, pl.ds(pl.multiple_of(k * 128, 128), 128), :], one_s.at[0], one_r.at[0], other
+    )
     swap.start()
+    drains.append(swap.wait_send)
+
+    def x_forward(t, _):
+        yi = (y + ring_step(t - 1)) % 8
+        for dx in (1, 3, 2):
+            xi = (x + dx) % 4
+            x_copy(xi, yi, x, 0).wait_recv()
+            f_copy(parity, xi, yi).start()
+        return 0
+
+    lax.fori_loop(0, 8, x_forward, 0)
 
     lane = lax.broadcasted_iota(jnp.int32, (128, 128), 1)
     sub = lax.broadcasted_iota(jnp.int32, (128, 128), 0)
@@ -305,34 +385,34 @@
             gram = jnp.where(spot, dotted, gram)
 
     swap.wait_recv()
-    for dx in range(4):
-        xi = (x + dx) % 4
-        if dx:
-
-            def x_wait(yi, _):
-                x_copy(xi, yi, x, 0).wait_recv()
-                return 0
-
-            lax.fori_loop(0, 8, x_wait, 0)
-        part = dot_nt(nb[xi], wb[xi].reshape(256, GROUP))
-        if dx:
-            kl[...] += part
-        else:
-            kl[...] = part
+    first = jnp.zeros((256, 128), F32)
+    for xi in range(4):
+        first = first + dot_nt(nb[xi], wb[xi, parity])
+    kl[parity] = first
+    second = jnp.zeros((256, 128), F32)
+    for xi in range(4):
+
+        def f_wait(yi, _):
+            f_copy(1 - parity, xi, yi).wait_recv()
+            return 0
+
+        lax.fori_loop(0, 8, f_wait, 0)
+        second = second + dot_nt(nb[xi], wb[xi, 1 - parity])
+    kl[1 - parity] = second
     mine = pl.ds(pl.multiple_of(k * 128, 128), 128)
     theirs = pl.ds(pl.multiple_of((1 - k) * 128, 128), 128)
-    kl_swap = rdma(kl.at[theirs], klr, one_s.at[1], one_r.at[1], other)
+    kl_swap = rdma(kl.at[:, theirs], klr, one_s.at[1], one_r.at[1], other)
     kl_swap.start()
+    drains.append(kl_swap.wait_send)
 
     def qu_wait(j, _):
-        qu_copy(j).wait_recv()
-        sg_copy(j).wait_recv()
-        return 0
-
-    lax.fori_loop(1, 9, qu_wait, 0)
+        for copy in qu_near(j):
+            copy.wait_recv()
+        return 0
+
+    lax.fori_loop(1, 8, qu_wait, 0)
     kl_swap.wait_recv()
-    both = kl[mine, :] + klr[...]
-    lin, tan = both[:, 0:128], both[:, 128:256]
+    lin, tan = kl[0, mine] + klr[0], kl[1, mine] + klr[1]
     cosine, sine = cs[0], cs[1]
     key_gain = kg[...]
 
@@ -403,6 +483,7 @@
     st_list = st_copies()
     for copy in st_list:
         copy.start()
+        drains.append(copy.wait_send)
     for copy in st_list:
         copy.wait_recv()
 
@@ -444,6 +525,7 @@
     cott[k] = jnp.transpose(cot).astype(BF16)
     cot_swap = rdma(cott.at[k], cott.at[k], one_s.at[2], one_r.at[2], other)
     cot_swap.start()
+    drains.append(cot_swap.wait_send)
     cot_in = rdma(cott.at[1 - k], cott.at[1 - k], one_s.at[2], one_r.at[2], other)
     cot_in.wait_recv()
     cots = jnp.concatenate([cott[0], cott[1]], axis=1)
@@ -458,15 +540,20 @@
         tb[dx] = dot_nn(cots, nb[(x + dx) % 4]).astype(BF16)
 
     def rx_send(t, _):
-        yi = (y + 4 + t) % 8
+        yi = (y + far_step(t)) % 8
         for dx in (2, 1, 3):
             rx_copy(dx, yi).start()
         return 0
 
     lax.fori_loop(0, 8, rx_send, 0)
-    kl_own = dot_nn(cots, nb[x])
-    tb_own = kl_own.astype(F32)
-    py[...] = tb_own
+
+    def rx_drain(yi, _):
+        for dx in (2, 1, 3):
+            rx_copy(dx, yi).wait_send()
+        return 0
+
+    drains.append(lambda: lax.fori_loop(0, 8, rx_drain, 0))
+    py[...] = dot_nn(cots, nb[x])
 
     def rx_sum(yi):
         cols = pl.ds(pl.multiple_of(yi * 16, 16), 16)
@@ -482,7 +569,7 @@
         return rdma(tb.at[0, cols], ry.at[dy], ry_s.at[dy - 1], ry_r.at[dy - 1], at_y(yi))
 
     def y_sum(t, _):
-        dy = (4 + t) % 8
+        dy = far_step(t)
         yi = (y + dy) % 8
         total = rx_sum(yi)
         cols = pl.ds(pl.multiple_of(yi * 16, 16), 16)
@@ -490,8 +577,13 @@
         ry_copy(t, dy).start()
         return 0
 
-    lax.fori_loop(0, 4, y_sum, 0)
-    lax.fori_loop(5, 8, y_sum, 0)
+    lax.fori_loop(0, 7, y_sum, 0)
+
+    def ry_drain(t, _):
+        ry_copy(0, t + 1).wait_send()
+        return 0
+
+    drains.append(lambda: lax.fori_loop(0, 7, ry_drain, 0))
     total = rx_sum(y)
 
     def y_add(dy, _):
@@ -534,6 +626,15 @@
 
     lax.fori_loop(0, 8, pz_send, 0)
 
+    def pz_drain(slot, _):
+        @pl.when(jnp.logical_not(pz_self(slot)))
+        def _():
+            pz_copy(slot, z).wait_send()
+
+        return 0
+
+    drains.append(lambda: lax.fori_loop(0, 8, pz_drain, 0))
+
     def rz_wait(t, _):
         src = (z + t) % 8
 
@@ -580,7 +681,7 @@
             copy(own, t, (own + far_step(t)) % 8).wait_send()
             return 0
 
-        lax.fori_loop(0, 7, drain, 0)
+        drains.append(lambda: lax.fori_loop(0, 7, drain, 0))
         return total
 
     sums = all_sum(0, sums, x * 2 + k, lambda i: (z * 8 + i, y))
@@ -596,55 +697,12 @@
     residual = product
     for a in range(7):
         residual = residual - coef[a : a + 1] * bas[a]
-    out[...] = residual / beta
-    aux[...] = jnp.where(sub8 < 7, coef, jnp.broadcast_to(beta, (8, 128)))
-
-    def g1_drain(t, _):
-        zi = (z + t) % 8
-
-        @pl.when(jnp.logical_or(zi != z, half != k))
-        def _():
-            g1_copy(zi, own_slot).wait_send()
-
-        return 0
-
-    lax.fori_loop(0, 8, g1_drain, 0)
-
-    def qu_drain(j, _):
-        qu_copy(j).wait_send()
-        sg_copy(j).wait_send()
-        return 0
-
-    lax.fori_loop(1, 9, qu_drain, 0)
-
-    def y_drain(t, _):
-        y_copy(y, (y + far_step(t)) % 8, t).wait_send()
-        ry_copy(0, t + 1).wait_send()
-        return 0
-
-    lax.fori_loop(0, 7, y_drain, 0)
-
-    def x_drain(yi, _):
-        for t, dx in enumerate((2, 1, 3)):
-            x_copy(x, yi, (x + dx) % 4, t).wait_send()
-            rx_copy(dx, yi).wait_send()
-        return 0
-
-    lax.fori_loop(0, 8, x_drain, 0)
-    swap.wait_send()
-    kl_swap.wait_send()
-    cot_swap.wait_send()
-    for copy in st_list:
-        copy.wait_send()
-
-    def pz_drain(slot, _):
-        @pl.when(jnp.logical_not(pz_self(slot)))
-        def _():
-            pz_copy(slot, z).wait_send()
-
-        return 0
-
-    lax.fori_loop(0, 8, pz_drain, 0)
+    out[...] = (residual / beta)[:, 0:ROWS]
+    coef_out[...] = coef_row[:, 0:7]
+    beta_out[...] = beta[:, 0:1]
+
+    for drain in drains:
+        drain()
 
 
 def body(
@@ -659,27 +717,24 @@
     direction,
     stored_basis,
 ):
-    tangent = (direction * D ** (-0.5)).astype(BF16)
-    pad = ((0, 0), (0, 0), (0, 128 - ROWS))
-    wt = jnp.pad(jnp.stack([key_weight.T, tangent.T]), pad)
-    stacked = jnp.concatenate([stored_basis, direction[None]], axis=0)
-    bas = jnp.pad(jnp.swapaxes(stacked, 1, 2), pad)
     dma = pltpu.SemaphoreType.DMA
     vmem = pl.BlockSpec(memory_space=pltpu.VMEM)
-    out, aux = pl.pallas_call(
+    out, coefficients, beta = pl.pallas_call(
         kernel,
-        out_shape=(jax.ShapeDtypeStruct((16, 128), F32), jax.ShapeDtypeStruct((8, 128), F32)),
-        in_specs=[vmem] * 10,
-        out_specs=(vmem, vmem),
+        out_shape=tuple(jax.ShapeDtypeStruct(shape, F32) for shape in ((16, ROWS), (1, 7), (1, 1))),
+        in_specs=[vmem] * 11,
+        out_specs=(vmem,) * 3,
         scratch_shapes=[
-            pltpu.VMEM((8, 2, 16, 128), BF16),
+            pltpu.VMEM((2, 16, 128), BF16),
+            pltpu.VMEM((7, 16, 128), F32),
+            pltpu.VMEM((8, 16, 128), BF16),
             pltpu.VMEM((4, 2, 128, GROUP), BF16),
             pltpu.VMEM((4, 256, GROUP), BF16),
             pltpu.VMEM((4, 128, GROUP), BF16),
             pltpu.VMEM((9, 2, 128, 128), BF16),
             pltpu.VMEM((9, 8, 128), jnp.int32),
-            pltpu.VMEM((256, 256), F32),
-            pltpu.VMEM((128, 256), F32),
+            pltpu.VMEM((2, 256, 128), F32),
+            pltpu.VMEM((2, 128, 128), F32),
             pltpu.VMEM((9, 128, 128), F32),
             pltpu.VMEM((9, 128, 128), F32),
             pltpu.VMEM((9, 128, 128), F32),
@@ -704,6 +759,8 @@
             dma((8,)),
             dma((3, 8)),
             dma((4, 8)),
+            dma((4, 8)),
+            dma((4, 8)),
             dma((3,)),
             dma((3,)),
             dma((16,)),
@@ -723,17 +780,18 @@
         name="lanczos_step",
     )(
         tokens[0],
-        norm_gain[None],
+        norm_gain.reshape(D // 128, 128),
         queries[0],
         values[0],
         upstream[0],
         segments,
-        wt,
+        key_weight.T,
+        direction.T,
         key_gain[None],
         jnp.asarray(FREQS),
-        bas,
+        jnp.swapaxes(stored_basis, 1, 2),
     )
-    return aux[:7, 0], aux[7, 0], out[:, :ROWS].T
+    return coefficients.reshape(7), beta.reshape(()), out.T
 
 
 def solution(mesh):

time: 107 us -> 94.1 us (0.88)
  Pallas kernels: 96.9 us -> 89 us
  local copies, waits for them, and re-layouts: 5.74 us -> 2.43 us
  other arithmetic: 2.81 us -> 0 us
  between operations: 0.64 us -> 2.41 us
    pallas_call x1, Pallas kernels: 96.9 us -> 89 us  [body(): pl.pallas_call(kernel, out_shape=tuple((jax.ShapeDtypeStruct(shape, F32)...]
    slice x2 -> x0, local copies, waits for them, and re-layouts: 2.5 us -> none  [body(): return (aux[:7, 0], aux[7, 0], out[:, :ROWS].T)]
    unnamed x0 -> x2, local copies, waits for them, and re-layouts: none -> 2.43 us
    another operation x2 -> x0, other arithmetic: 1.99 us -> none  [body(): wt = jnp.pad(jnp.stack([key_weight.T, tangent.T]), pad)]
    broadcast_in_dim x1 -> x0, local copies, waits for them, and re-layouts: 1.32 us -> none  [body(): norm_gain[None]]
    transpose x1 -> x0, local copies, waits for them, and re-layouts: 1.29 us -> none  [body(): return (aux[:7, 0], aux[7, 0], out[:, :ROWS].T)]
where the time goes in v2:
time: 94.1 us; the launch traced here: 93.9 us
  Pallas kernels  89 us (95%)
  local copies, waits for them, and re-layouts  2.43 us (3%)
  between operations  2.41 us (3%)
    pallas_call x1, Pallas kernels, body(): pl.pallas_call(kernel, out_shape=tuple((jax.ShapeDtypeStruct(shape, F32)...  89 us
    unnamed x2, local copies, waits for them, and re-layouts  2.43 us

profile of v2, /device:TPU:1, one launch (start us, length us, event | category | flops | bytes accessed | tf_op | source)
XLA Modules:
  0.0 93.9 jit_solution(2505798397723394960)
XLA Ops:
  0.6 89.0 %lanczos_step.1 = (f32[16,84]{1,0:T(8,128)}, f32[1,7]{1,0:T(1,128)}, f32[1,1]{1,0:T(1,128)}) custom-call(bf16[128,5376]{1,0:T(8,128)(2,1)} %bitcast.12, bf16[42,128]{1,0:T(8,128)(2,1)} %bitcast.17, bf16[128,128]{1,0:T(8,128)(2,1)} %bitcast.14, bf16[128,128]{1,0:T(8,128)(2,1)} %bitcast.15, bf16[128,128]{1,0:T(8,128)(2,1)} %bitcast.16, s32[1,128]{1,0:T(1,128)} %seg_in.1, ...), custom_call_target="tpu_custom_call" | custom-call | tf_op jit(solution)/shard_map/lanczos_step/pallas_call | solution.py:722
  89.7 1.1 %copy.17 = f32[7]{0:T(128)} copy(f32[7]{0:T(128)} %bitcast.22) | data formatting | bytes 56
  91.5 1.3 %copy.19 = f32[84,16]{0,1:T(8,128)} copy(f32[84,16]{0,1:T(8,128)} %bitcast.19) | data formatting | bytes 10752

commit v3 on v2

--- a/solution.py
+++ b/solution.py
@@ -15,6 +15,7 @@
 EPSILON = 1e-06
 ENTRIES = D * HD
 GROUP = 768
+CUT = 512
 LOW = -1e30
 MESH = pl.DeviceIdType.MESH
 F32 = jnp.float32
@@ -22,6 +23,28 @@
 FREQS = np.tile(10000.0 ** (-np.arange(64) / 64.0), 2)[None].astype(np.float32)
 
 
+def placement(xi):
+    spans = {}
+    for zi in range(4):
+        start = (zi * 672 + xi * 168) % 128
+        for m in range((start + 167) // 128 + 1):
+            spans[zi, m] = (max(start - 128 * m, 0), min(start + 168 - 128 * m, 128))
+    heads = sorted((span[1], key) for key, span in spans.items() if span[0] == 0 and span[1] < 128)
+    tails = sorted((span[0], key) for key, span in spans.items() if span[0] > 0)
+    tiles, free = {}, 0
+    for end, key in reversed(heads):
+        fits = [tail for tail in tails if tail[0] >= end]
+        tiles[key] = free
+        if fits:
+            tails.remove(fits[0])
+            tiles[fits[0][1]] = free
+        free += 1
+    for key in [tail[1] for tail in tails] + [key for key, span in spans.items() if span == (0, 128)]:
+        tiles[key] = free
+        free += 1
+    return spans, tiles
+
+
 def dot_nt(a, b):
     return lax.dot_general(a, b, (((1,), (1,)), ((), ())), preferred_element_type=F32)
 
@@ -45,7 +68,7 @@
 
 
 def kernel(
-    tok,
+    tok_in,
     gain,
     q_in,
     v_in,
@@ -59,6 +82,7 @@
     out,
     coef_out,
     beta_out,
+    tok,
     wt,
     bas,
     g1,
@@ -75,10 +99,13 @@
     rst,
     cott,
     acc,
+    ta,
     tb,
     rx,
     py,
     ry,
+    sy,
+    sx,
     pz,
     rz,
     ar,
@@ -97,12 +124,17 @@
     f_r,
     one_s,
     one_r,
+    tok_s,
     st_s,
     st_r,
     rx_s,
     rx_r,
     ry_s,
     ry_r,
+    sy_s,
+    sy_r,
+    sx_s,
+    sx_r,
     rz_s,
     rz_r,
     ar_s,
@@ -116,7 +148,6 @@
     half = z // 4
     zz = z % 4
     parity = z % 2
-    place = ctx % 8
 
     def at_z(zi, ki):
         return ((zi * 4 + x) * 2 + ki, y)
@@ -132,6 +163,11 @@
 
     other = ((z * 4 + x) * 2 + (1 - k), y)
     drains = []
+
+    def finish():
+        while drains:
+            drains.pop()()
+
 
     def rdma(src, dst, send, recv, device):
         return pltpu.make_async_remote_copy(
@@ -142,6 +178,9 @@
             device_id=device,
             device_id_type=MESH,
         )
+
+    tok_copy = pltpu.make_async_copy(tok_in, tok, tok_s)
+    tok_copy.start()
 
     barrier = pltpu.get_barrier_semaphore()
 
@@ -208,13 +247,20 @@
             for ref, sends, recvs in ((qu, qu_s, qu_r), (segb, sg_s, sg_r))
         ]
 
-    def qu_near(j):
-        source = 8 * ((j + 7 - place) // 8)
-        device = at_ctx(ctx + source + 64 - j)
+    def qu_pair(source, j, device):
         return [
             rdma(ref.at[source], ref.at[j], sends.at[j - 1], recvs.at[j - 1], device)
             for ref, sends, recvs in ((qu, qu_s, qu_r), (segb, sg_s, sg_r))
         ]
+
+    def qu_chip(dx):
+        return qu_pair(8 * (1 - (x + dx) // 4), 8 - 2 * dx, at_x((x + dx) % 4))
+
+    def qu_core():
+        return qu_pair(8 * (1 - k), 7 - 6 * k, other)
+
+    def qu_next(dx):
+        return qu_pair(8 - 2 * dx, 7 - 2 * dx + 2 * k, other)
 
     for copy in qu_far():
         copy.start()
@@ -231,24 +277,16 @@
         normed = floats * scale * gain_row
         for hh in range(2):
             for xi in range(4):
-                tiles = [jnp.zeros((16, 128), F32) for _ in range(6)]
-                for zi in range(4):
-                    start = hh * HALF + zi * 672 + xi * 168
-                    first = min(start // 128, D // 128 - 3)
-                    shift = start - first * 128
-                    goal, lead = (168 * zi) // 128, (168 * zi) % 128
-                    slab = normed[:, first * 128 : first * 128 + 384]
-                    moved = pltpu.roll(slab, (lead - shift) % 384, 1) if lead != shift else slab
-                    for m in range(3):
-                        low, high = lead - 128 * m, lead + 168 - 128 * m
-                        if high <= 0 or low >= 128:
-                            continue
-                        part = moved[:, 128 * m : 128 * m + 128]
-                        if low > 0 or high < 128:
-                            inside = jnp.logical_and(lane128 >= low, lane128 < high)
-                            part = jnp.where(inside, part, 0.0)
-                        tiles[goal + m] = tiles[goal + m] + part
-                group = jnp.concatenate(tiles, axis=1).astype(BF16)
+                spans, tiles = placement(xi)
+                columns = [None] * 6
+                for key, (low, high) in spans.items():
+                    source = (hh * HALF + key[0] * 672 + xi * 168) // 128 + key[1]
+                    part = normed[:, source * 128 : source * 128 + 128]
+                    held = columns[tiles[key]]
+                    if held is not None:
+                        part = jnp.where(lane128 < high, part, held) if low == 0 else jnp.where(lane128 >= low, part, held)
+                    columns[tiles[key]] = part
+                group = jnp.concatenate(columns, axis=1).astype(BF16)
 
                 @pl.when(k == hh)
                 def _():
@@ -258,7 +296,19 @@
                 def _():
                     ns[xi, rows, :] = group
 
-    norm_chunk(7)
+    tok_copy.wait()
+
+    def norm(r, _):
+        norm_chunk(r)
+        return 0
+
+    lax.fori_loop(0, 8, norm, 0)
+    swap = rdma(
+        ns, nb.at[:, pl.ds(pl.multiple_of(k * 128, 128), 128), :], one_s.at[0], one_r.at[0], other
+    )
+    swap.start()
+    drains.append(swap.wait_send)
+
 
     def g1_wait(slot, _):
         zi = half * 0 + k * 4 + slot // 2
@@ -271,15 +321,24 @@
         return 0
 
     lax.fori_loop(0, 8, g1_wait, 0)
-    tiles = [jnp.zeros((16, 128), F32) for _ in range(6)]
-    for slot in range(8):
-        piece = g1[slot].astype(F32)
-        goal, lead = (ROWS * slot) // 128, (ROWS * slot) % 128
-        moved = pltpu.roll(piece, lead, 1) if lead else piece
-        tiles[goal] = tiles[goal] + jnp.where(lane128 >= lead, moved, 0.0)
-        if lead + ROWS > 128:
-            tiles[goal + 1] = tiles[goal + 1] + jnp.where(lane128 < lead, moved, 0.0)
-    wb[x, parity, pl.ds(pl.multiple_of(y * 16, 16), 16), :] = jnp.concatenate(tiles, axis=1).astype(BF16)
+    for xi in range(4):
+
+        @pl.when(x == xi)
+        def _():
+            tiles = placement(xi)[1]
+            columns = [jnp.zeros((16, 128), F32) for _ in range(6)]
+            for slot in range(8):
+                piece = g1[slot].astype(F32)
+                start = (slot // 2 * 672 + xi * 168) % 128 + slot % 2 * ROWS
+                m, lead = start // 128, start % 128
+                moved = pltpu.roll(piece, lead, 1) if lead else piece
+                tile = tiles[slot // 2, m]
+                columns[tile] = columns[tile] + jnp.where(lane128 >= lead, moved, 0.0)
+                if lead + ROWS > 128:
+                    tile = tiles[slot // 2, m + 1]
+                    columns[tile] = columns[tile] + jnp.where(lane128 < lead, moved, 0.0)
+            own = pl.ds(pl.multiple_of(y * 16, 16), 16)
+            wb[xi, parity, own, :] = jnp.concatenate(columns, axis=1).astype(BF16)
 
     def piece_at(matrix, xi, yi):
         return wb.at[xi, matrix, pl.ds(pl.multiple_of(yi * 16, 16), 16), :]
@@ -315,31 +374,31 @@
         f_copy(parity, x, yi).start()
 
     x_send(y)
-    for copy in qu_far():
-        copy.wait_recv()
-
-    def qu_send(j, _):
-        for copy in qu_near(j):
-            copy.start()
-        return 0
-
-    lax.fori_loop(1, 8, qu_send, 0)
-
-    def qu_drain(j, _):
-        for copy in qu_near(j):
-            copy.wait_send()
-        return 0
-
-    drains.append(lambda: lax.fori_loop(1, 8, qu_drain, 0))
+    lane = lax.broadcasted_iota(jnp.int32, (128, 128), 1)
+    sub = lax.broadcasted_iota(jnp.int32, (128, 128), 0)
+    angle = (ctx * 128 + sub).astype(F32) * freq_in[...]
+    cs[0] = jnp.cos(angle)
+    cs[1] = jnp.sin(angle) * jnp.where(lane < 64, -1.0, 1.0)
+    key_doc = jnp.transpose(jnp.broadcast_to(segb[0, 0:1].astype(F32), (128, 128)))
 
     def y_forward(t, _):
-        norm_chunk(t)
         src = (y + ring_step(t)) % 8
         y_copy(src, y, 0).wait_recv()
         x_send(src)
         return 0
 
     lax.fori_loop(0, 7, y_forward, 0)
+
+    for copy in qu_far():
+        copy.wait_recv()
+
+    for dx in (2, 1, 3):
+        for copy in qu_chip(dx):
+            copy.start()
+            drains.append(copy.wait_send)
+    for copy in qu_core():
+        copy.start()
+        drains.append(copy.wait_send)
 
     def x_drain(yi, _):
         for t, dx in enumerate((2, 1, 3)):
@@ -349,12 +408,6 @@
         return 0
 
     drains.append(lambda: lax.fori_loop(0, 8, x_drain, 0))
-
-    swap = rdma(
-        ns, nb.at[:, pl.ds(pl.multiple_of(k * 128, 128), 128), :], one_s.at[0], one_r.at[0], other
-    )
-    swap.start()
-    drains.append(swap.wait_send)
 
     def x_forward(t, _):
         yi = (y + ring_step(t - 1)) % 8
@@ -366,23 +419,12 @@
 
     lax.fori_loop(0, 8, x_forward, 0)
 
-    lane = lax.broadcasted_iota(jnp.int32, (128, 128), 1)
-    sub = lax.broadcasted_iota(jnp.int32, (128, 128), 0)
-    angle = (ctx * 128 + sub).astype(F32) * freq_in[...]
-    cs[0] = jnp.cos(angle)
-    cs[1] = jnp.sin(angle) * jnp.where(lane < 64, -1.0, 1.0)
-    key_doc = jnp.transpose(jnp.broadcast_to(segb[0, 0:1].astype(F32), (128, 128)))
-
-    lane8 = lax.broadcasted_iota(jnp.int32, (8, 128), 1)
-    sub8 = lax.broadcasted_iota(jnp.int32, (8, 128), 0)
-    gram = jnp.zeros((8, 128), F32)
-    for a in range(7):
-        for b in range(a, 7):
-            dotted = jnp.sum(jnp.sum(bas[a] * bas[b], axis=0, keepdims=True), axis=1, keepdims=True)
-            spot = jnp.logical_and(sub8 == a, lane8 == b)
-            if a != b:
-                spot = jnp.logical_or(spot, jnp.logical_and(sub8 == b, lane8 == a))
-            gram = jnp.where(spot, dotted, gram)
+    for dx in (1, 3, 2):
+        for copy in qu_chip(dx):
+            copy.wait_recv()
+        for copy in qu_next(dx):
+            copy.start()
+            drains.append(copy.wait_send)
 
     swap.wait_recv()
     first = jnp.zeros((256, 128), F32)
@@ -405,12 +447,9 @@
     kl_swap.start()
     drains.append(kl_swap.wait_send)
 
-    def qu_wait(j, _):
-        for copy in qu_near(j):
+    for j in range(1, 8, 2):
+        for copy in qu_pair(0, j, other):
             copy.wait_recv()
-        return 0
-
-    lax.fori_loop(1, 8, qu_wait, 0)
     kl_swap.wait_recv()
     lin, tan = kl[0, mine] + klr[0], kl[1, mine] + klr[1]
     cosine, sine = cs[0], cs[1]
@@ -454,7 +493,8 @@
         gv[j] = g
         return 0
 
-    lax.fori_loop(0, 9, score, 0)
+    for j in range(9):
+        score(j, 0)
 
     def st_copies():
         copies = []
@@ -484,6 +524,17 @@
     for copy in st_list:
         copy.start()
         drains.append(copy.wait_send)
+    lane8 = lax.broadcasted_iota(jnp.int32, (8, 128), 1)
+    sub8 = lax.broadcasted_iota(jnp.int32, (8, 128), 0)
+    gram = jnp.zeros((8, 128), F32)
+    for a in range(7):
+        for b in range(a, 7):
+            dotted = jnp.sum(jnp.sum(bas[a] * bas[b], axis=0, keepdims=True), axis=1, keepdims=True)
+            spot = jnp.logical_and(sub8 == a, lane8 == b)
+            if a != b:
+                spot = jnp.logical_or(spot, jnp.logical_and(sub8 == b, lane8 == a))
+            gram = jnp.where(spot, dotted, gram)
+
     for copy in st_list:
         copy.wait_recv()
 
@@ -510,7 +561,8 @@
         return 0
 
     acc[...] = jnp.zeros((256, 128), F32)
-    lax.fori_loop(0, 9, gradient, 0)
+    for j in range(9):
+        gradient(j, 0)
 
     w = rope_back(acc[0:128] * SCORE_SCALE) * key_gain
     w_tan = rope_back(acc[128:256] * SCORE_SCALE) * key_gain
@@ -530,22 +582,37 @@
     cot_in.wait_recv()
     cots = jnp.concatenate([cott[0], cott[1]], axis=1)
 
+    def slice_of(yi):
+        return pl.ds(pl.multiple_of(yi * 16, 16), 16)
+
     def rx_copy(dx, yi):
-        cols = pl.ds(pl.multiple_of(yi * 16, 16), 16)
+        cols = slice_of(yi)
         return rdma(
-            tb.at[dx, cols], rx.at[dx - 1, cols], rx_s.at[dx - 1, yi], rx_r.at[dx - 1, yi], at_x((x + dx) % 4)
+            ta.at[dx, cols], rx.at[dx - 1, cols], rx_s.at[dx - 1, yi], rx_r.at[dx - 1, yi], at_x((x + dx) % 4)
         )
 
+    def sy_copy(dy):
+        yi = (y + dy) % 8
+        return rdma(tb.at[:, slice_of(yi)], sy.at[dy], sy_s.at[dy - 1], sy_r.at[dy - 1], at_y(yi))
+
+    for dx in range(4):
+        part = dot_nn(cots, nb[(x + dx) % 4])
+        if dx:
+            ta[dx] = part[:, 0:CUT].astype(BF16)
+        else:
+            py[...] = part
+        tb[dx] = part[:, CUT:GROUP].astype(BF16)
+
+    def rx_send(t, _):
+        dy = far_step(t)
+        sy_copy(dy).start()
+        for dx in (2, 1, 3):
+            rx_copy(dx, (y + dy) % 8).start()
+        return 0
+
+    lax.fori_loop(0, 7, rx_send, 0)
     for dx in (2, 1, 3):
-        tb[dx] = dot_nn(cots, nb[(x + dx) % 4]).astype(BF16)
-
-    def rx_send(t, _):
-        yi = (y + far_step(t)) % 8
-        for dx in (2, 1, 3):
-            rx_copy(dx, yi).start()
-        return 0
-
-    lax.fori_loop(0, 8, rx_send, 0)
+        rx_copy(dx, y).start()
 
     def rx_drain(yi, _):
         for dx in (2, 1, 3):
@@ -553,60 +620,87 @@
         return 0
 
     drains.append(lambda: lax.fori_loop(0, 8, rx_drain, 0))
-    py[...] = dot_nn(cots, nb[x])
 
     def rx_sum(yi):
-        cols = pl.ds(pl.multiple_of(yi * 16, 16), 16)
-        total = py[cols, :]
-        for dx in (2, 1, 3):
+        cols = slice_of(yi)
+        total = py[cols, 0:CUT]
+        for dx in (1, 3, 2):
             rx_copy(dx, yi).wait_recv()
             total = total + rx[dx - 1, cols, :].astype(F32)
         return total
 
-    def ry_copy(t, dy):
+    def ry_copy(dy):
         yi = (y + dy) % 8
-        cols = pl.ds(pl.multiple_of(yi * 16, 16), 16)
-        return rdma(tb.at[0, cols], ry.at[dy], ry_s.at[dy - 1], ry_r.at[dy - 1], at_y(yi))
+        return rdma(ta.at[0, slice_of(yi)], ry.at[dy], ry_s.at[dy - 1], ry_r.at[dy - 1], at_y(yi))
 
     def y_sum(t, _):
         dy = far_step(t)
         yi = (y + dy) % 8
-        total = rx_sum(yi)
-        cols = pl.ds(pl.multiple_of(yi * 16, 16), 16)
-        tb[0, cols, :] = total.astype(BF16)
-        ry_copy(t, dy).start()
+        ta[0, slice_of(yi), :] = rx_sum(yi).astype(BF16)
+        ry_copy(dy).start()
         return 0
 
     lax.fori_loop(0, 7, y_sum, 0)
 
+    def sy_wait(t, _):
+        sy_copy(ring_step(t)).wait_recv()
+        return 0
+
+    lax.fori_loop(0, 7, sy_wait, 0)
+
+    def sx_copy(dx):
+        return rdma(sx.at[dx], sx.at[3 + dx], sx_s.at[dx - 1], sx_r.at[dx - 1], at_x((x + dx) % 4))
+
+    for dx in (2, 1, 3, 0):
+        part = tb[dx, slice_of(y), :].astype(F32) if dx else py[slice_of(y), CUT:GROUP]
+        for dy in range(1, 8):
+            part = part + sy[dy, dx].astype(F32)
+        if dx:
+            sx[dx] = part.astype(BF16)
+            sx_copy(dx).start()
+            drains.append(sx_copy(dx).wait_send)
+    total_a = rx_sum(y)
+
+    def ry_wait(t, _):
+        ry_copy(ring_step(t)).wait_recv()
+        return 0
+
+    lax.fori_loop(0, 7, ry_wait, 0)
+    for dy in range(1, 8):
+        total_a = total_a + ry[dy].astype(F32)
+    for dx in (1, 3, 2):
+        sx_copy(dx).wait_recv()
+        part = part + sx[3 + dx].astype(F32)
+    total = jnp.concatenate([total_a, part], axis=1)
+
     def ry_drain(t, _):
-        ry_copy(0, t + 1).wait_send()
+        ry_copy(t + 1).wait_send()
+        sy_copy(t + 1).wait_send()
         return 0
 
     drains.append(lambda: lax.fori_loop(0, 7, ry_drain, 0))
-    total = rx_sum(y)
-
-    def y_add(dy, _):
-        ry_copy(0, dy).wait_recv()
-        return 0
-
-    lax.fori_loop(1, 8, y_add, 0)
-    for dy in range(1, 8):
-        total = total + ry[dy].astype(F32)
 
     def pz_copy(slot, src_z):
         zi = k * 4 + slot // 2
         return rdma(pz.at[slot], rz.at[src_z], rz_s.at[slot], rz_r.at[src_z], at_z(zi, slot % 2))
 
-    for slot in range(8):
-        goal, lead = (ROWS * slot) // 128, (ROWS * slot) % 128
-        piece = total[:, goal * 128 : goal * 128 + 128]
-        if lead:
-            piece = pltpu.roll(piece, 128 - lead, 1)
-        if lead + ROWS > 128:
-            following = pltpu.roll(total[:, goal * 128 + 128 : goal * 128 + 256], 128 - lead, 1)
-            piece = jnp.where(lane128 < 128 - lead, piece, following)
-        pz[slot] = jnp.where(lane128 < ROWS, piece, 0.0)
+    for xi in range(4):
+
+        @pl.when(x == xi)
+        def _():
+            tiles = placement(xi)[1]
+            for slot in range(8):
+                start = (slot // 2 * 672 + xi * 168) % 128 + slot % 2 * ROWS
+                m, lead = start // 128, start % 128
+                tile = tiles[slot // 2, m]
+                piece = total[:, tile * 128 : tile * 128 + 128]
+                if lead:
+                    piece = pltpu.roll(piece, 128 - lead, 1)
+                if lead + ROWS > 128:
+                    tile = tiles[slot // 2, m + 1]
+                    following = pltpu.roll(total[:, tile * 128 : tile * 128 + 128], 128 - lead, 1)
+                    piece = jnp.where(lane128 < 128 - lead, piece, following)
+                pz[slot] = jnp.where(lane128 < ROWS, piece, 0.0)
 
     def pz_self(slot):
         return jnp.logical_and(k * 4 + slot // 2 == z, slot % 2 == k)
@@ -667,6 +761,7 @@
             return 0
 
         lax.fori_loop(0, 7, send, 0)
+        finish()
 
         def wait(t, _):
             copy((own + ring_step(t)) % 8, 0, own).wait_recv()
@@ -701,8 +796,7 @@
     coef_out[...] = coef_row[:, 0:7]
     beta_out[...] = beta[:, 0:1]
 
-    for drain in drains:
-        drain()
+    finish()
 
 
 def body(
@@ -722,9 +816,10 @@
     out, coefficients, beta = pl.pallas_call(
         kernel,
         out_shape=tuple(jax.ShapeDtypeStruct(shape, F32) for shape in ((16, ROWS), (1, 7), (1, 1))),
-        in_specs=[vmem] * 11,
+        in_specs=[pl.BlockSpec(memory_space=pl.ANY)] + [vmem] * 10,
         out_specs=(vmem,) * 3,
         scratch_shapes=[
+            pltpu.VMEM((128, D), BF16),
             pltpu.VMEM((2, 16, 128), BF16),
             pltpu.VMEM((7, 16, 128), F32),
             pltpu.VMEM((8, 16, 128), BF16),
@@ -741,10 +836,13 @@
             pltpu.VMEM((17, 9, 8, 128), F32),
             pltpu.VMEM((2, 128, 128), BF16),
             pltpu.VMEM((256, 128), F32),
-            pltpu.VMEM((4, 128, GROUP), BF16),
-            pltpu.VMEM((3, 128, GROUP), BF16),
+            pltpu.VMEM((4, 128, CUT), BF16),
+            pltpu.VMEM((4, 128, GROUP - CUT), BF16),
+            pltpu.VMEM((3, 128, CUT), BF16),
             pltpu.VMEM((128, GROUP), F32),
-            pltpu.VMEM((8, 16, GROUP), BF16),
+            pltpu.VMEM((8, 16, CUT), BF16),
+            pltpu.VMEM((8, 4, 16, GROUP - CUT), BF16),
+            pltpu.VMEM((7, 16, GROUP - CUT), BF16),
             pltpu.VMEM((8, 16, 128), F32),
             pltpu.VMEM((8, 16, 128), F32),
             pltpu.VMEM((3, 8, 16, 128), F32),
@@ -763,12 +861,17 @@
             dma((4, 8)),
             dma((3,)),
             dma((3,)),
+            dma,
             dma((16,)),
             dma((16,)),
             dma((3, 8)),
             dma((3, 8)),
             dma((7,)),
             dma((7,)),
+            dma((7,)),
+            dma((7,)),
+            dma((3,)),
+            dma((3,)),
             dma((8,)),
             dma((8,)),
             dma((3, 7)),

time: 94.1 us -> 88.6 us (0.942)
  Pallas kernels: 89 us -> 83.5 us
    pallas_call x1, Pallas kernels: 89 us -> 83.5 us  [body(): pl.pallas_call(kernel, out_shape=tuple((jax.ShapeDtypeStruct(shape, F32)...]
where the time goes in v3:
time: 88.6 us; the launch traced here: 88.3 us
  Pallas kernels  83.5 us (94%)
  local copies, waits for them, and re-layouts  2.43 us (3%)
  between operations  2.41 us (3%)
    pallas_call x1, Pallas kernels, body(): pl.pallas_call(kernel, out_shape=tuple((jax.ShapeDtypeStruct(shape, F32)...  83.5 us
    unnamed x2, local copies, waits for them, and re-layouts  2.43 us

profile of v3, /device:TPU:1, one launch (start us, length us, event | category | flops | bytes accessed | tf_op | source)
XLA Modules:
  0.0 88.3 jit_solution(3873141181410000648)
XLA Ops:
  0.6 83.5 %lanczos_step.1 = (f32[16,84]{1,0:T(8,128)}, f32[1,7]{1,0:T(1,128)}, f32[1,1]{1,0:T(1,128)}) custom-call(bf16[128,5376]{1,0:T(8,128)(2,1)} %bitcast.12, bf16[42,128]{1,0:T(8,128)(2,1)} %bitcast.17, bf16[128,128]{1,0:T(8,128)(2,1)} %bitcast.14, bf16[128,128]{1,0:T(8,128)(2,1)} %bitcast.15, bf16[128,128]{1,0:T(8,128)(2,1)} %bitcast.16, s32[1,128]{1,0:T(1,128)} %seg_in.1, ...), custom_call_target="tpu_custom_call" | custom-call | tf_op jit(solution)/shard_map/lanczos_step/pallas_call | solution.py:816
  84.1 1.1 %copy.17 = f32[7]{0:T(128)} copy(f32[7]{0:T(128)} %bitcast.22) | data formatting | bytes 56
  85.9 1.3 %copy.19 = f32[84,16]{0,1:T(8,128)} copy(f32[84,16]{0,1:T(8,128)} %bitcast.19) | data formatting | bytes 10752

commit v4 on v3

--- a/solution.py
+++ b/solution.py
@@ -69,20 +69,28 @@
 
 def kernel(
     tok_in,
-    gain,
+    gain_in,
     q_in,
     v_in,
     u_in,
     seg_in,
     w_in,
     dir_in,
-    kg,
+    kg_in,
     freq_in,
     bas_in,
     out,
     coef_out,
     beta_out,
     tok,
+    gain,
+    v_own,
+    seg_own,
+    w_own,
+    dir_own,
+    kg,
+    freq,
+    bas_own,
     wt,
     bas,
     g1,
@@ -124,7 +132,7 @@
     f_r,
     one_s,
     one_r,
-    tok_s,
+    in_s,
     st_s,
     st_r,
     rx_s,
@@ -179,31 +187,48 @@
             device_id_type=MESH,
         )
 
-    tok_copy = pltpu.make_async_copy(tok_in, tok, tok_s)
-    tok_copy.start()
-
     barrier = pltpu.get_barrier_semaphore()
 
     def greet(device):
         pl.semaphore_signal(barrier, inc=1, device_id=device, device_id_type=MESH)
 
-    for d in range(1, 9):
-        greet(at_ctx(ctx + d))
-        greet(at_ctx(ctx + 64 - d))
-    for dz in range(2, 7):
+    for dz in (4, 3, 5, 2, 6):
         greet(at_z((z + dz) % 8, 0))
         greet(at_z((z + dz) % 8, 1))
     for dz in (1, 7):
         greet(at_z((z + dz) % 8, 1 - k))
-    for dy in range(1, 8):
+    for dy in (4, 3, 5, 2, 6, 1, 7):
         greet(at_y((y + dy) % 8))
-
-    qu[0, 0] = q_in[...]
-    qu[0, 1] = u_in[...]
-    segb[0] = jnp.broadcast_to(seg_in[...], (8, 128))
+    for d in range(8, 0, -1):
+        greet(at_ctx(ctx + d))
+        greet(at_ctx(ctx + 64 - d))
+
+    fetches = [
+        pltpu.make_async_copy(source, target, in_s.at[i])
+        for i, (source, target) in enumerate(
+            (
+                (w_in, w_own),
+                (dir_in, dir_own),
+                (q_in, qu.at[0, 0]),
+                (u_in, qu.at[0, 1]),
+                (seg_in, seg_own),
+                (tok_in, tok),
+                (gain_in, gain),
+                (v_in, v_own),
+                (kg_in, kg),
+                (freq_in, freq),
+                (bas_in, bas_own),
+            )
+        )
+    ]
+    for fetch in fetches:
+        fetch.start()
     wt[...] = jnp.zeros((2, 16, 128), BF16)
-    wt[0, :, 0:ROWS] = w_in[...]
-    wt[1, :, 0:ROWS] = (dir_in[...] * D ** (-0.5)).astype(BF16)
+    bas[...] = jnp.zeros((7, 16, 128), F32)
+    for fetch in fetches[:2]:
+        fetch.wait()
+    wt[0, :, 0:ROWS] = w_own[...]
+    wt[1, :, 0:ROWS] = (dir_own[...] * D ** (-0.5)).astype(BF16)
     pl.semaphore_wait(barrier, 35)
 
     own_slot = zz * 2 + k
@@ -237,9 +262,9 @@
     def _():
         g1[own_slot] = wt[parity]
 
-    bas[...] = jnp.zeros((7, 16, 128), F32)
-    bas[0:6, :, 0:ROWS] = bas_in[...]
-    bas[6, :, 0:ROWS] = dir_in[...]
+    for fetch in fetches[2:]:
+        fetch.wait()
+    segb[0] = jnp.broadcast_to(seg_own[...], (8, 128))
 
     def qu_far():
         return [
@@ -296,7 +321,6 @@
                 def _():
                     ns[xi, rows, :] = group
 
-    tok_copy.wait()
 
     def norm(r, _):
         norm_chunk(r)
@@ -376,7 +400,7 @@
     x_send(y)
     lane = lax.broadcasted_iota(jnp.int32, (128, 128), 1)
     sub = lax.broadcasted_iota(jnp.int32, (128, 128), 0)
-    angle = (ctx * 128 + sub).astype(F32) * freq_in[...]
+    angle = (ctx * 128 + sub).astype(F32) * freq[...]
     cs[0] = jnp.cos(angle)
     cs[1] = jnp.sin(angle) * jnp.where(lane < 64, -1.0, 1.0)
     key_doc = jnp.transpose(jnp.broadcast_to(segb[0, 0:1].astype(F32), (128, 128)))
@@ -388,6 +412,25 @@
         return 0
 
     lax.fori_loop(0, 7, y_forward, 0)
+
+    def x_drain(yi, _):
+        for t, dx in enumerate((2, 1, 3)):
+            x_copy(x, yi, (x + dx) % 4, t).wait_send()
+        for xi in range(4):
+            f_copy(parity, xi, yi).wait_send()
+        return 0
+
+    drains.append(lambda: lax.fori_loop(0, 8, x_drain, 0))
+
+    def x_forward(t, _):
+        yi = (y + ring_step(t - 1)) % 8
+        for dx in (1, 3, 2):
+            xi = (x + dx) % 4
+            x_copy(xi, yi, x, 0).wait_recv()
+            f_copy(parity, xi, yi).start()
+        return 0
+
+    lax.fori_loop(0, 8, x_forward, 0)
 
     for copy in qu_far():
         copy.wait_recv()
@@ -399,32 +442,6 @@
     for copy in qu_core():
         copy.start()
         drains.append(copy.wait_send)
-
-    def x_drain(yi, _):
-        for t, dx in enumerate((2, 1, 3)):
-            x_copy(x, yi, (x + dx) % 4, t).wait_send()
-        for xi in range(4):
-            f_copy(parity, xi, yi).wait_send()
-        return 0
-
-    drains.append(lambda: lax.fori_loop(0, 8, x_drain, 0))
-
-    def x_forward(t, _):
-        yi = (y + ring_step(t - 1)) % 8
-        for dx in (1, 3, 2):
-            xi = (x + dx) % 4
-            x_copy(xi, yi, x, 0).wait_recv()
-            f_copy(parity, xi, yi).start()
-        return 0
-
-    lax.fori_loop(0, 8, x_forward, 0)
-
-    for dx in (1, 3, 2):
-        for copy in qu_chip(dx):
-            copy.wait_recv()
-        for copy in qu_next(dx):
-            copy.start()
-            drains.append(copy.wait_send)
 
     swap.wait_recv()
     first = jnp.zeros((256, 128), F32)
@@ -446,6 +463,12 @@
     kl_swap = rdma(kl.at[:, theirs], klr, one_s.at[1], one_r.at[1], other)
     kl_swap.start()
     drains.append(kl_swap.wait_send)
+    for dx in (1, 3, 2):
+        for copy in qu_chip(dx):
+            copy.wait_recv()
+        for copy in qu_next(dx):
+            copy.start()
+            drains.append(copy.wait_send)
 
     for j in range(1, 8, 2):
         for copy in qu_pair(0, j, other):
@@ -472,7 +495,7 @@
     k_high, k_low = split(keyed)
     t_high, t_low = split(keyed_tan)
     stacked_keys = jnp.concatenate([k_high, k_low, t_high, t_low], axis=0)
-    value_rows = v_in[...]
+    value_rows = v_own[...]
 
     def score(j, _):
         raw = dot_nt(stacked_keys, qu[j, 0])
@@ -498,7 +521,7 @@
 
     def st_copies():
         copies = []
-        for d in range(1, 9):
+        for d in (8, 7, 6, 5, 4, 3, 2, 1):
             n = 9 - d
             copies.append(
                 rdma(
@@ -524,17 +547,7 @@
     for copy in st_list:
         copy.start()
         drains.append(copy.wait_send)
-    lane8 = lax.broadcasted_iota(jnp.int32, (8, 128), 1)
-    sub8 = lax.broadcasted_iota(jnp.int32, (8, 128), 0)
-    gram = jnp.zeros((8, 128), F32)
-    for a in range(7):
-        for b in range(a, 7):
-            dotted = jnp.sum(jnp.sum(bas[a] * bas[b], axis=0, keepdims=True), axis=1, keepdims=True)
-            spot = jnp.logical_and(sub8 == a, lane8 == b)
-            if a != b:
-                spot = jnp.logical_or(spot, jnp.logical_and(sub8 == b, lane8 == a))
-            gram = jnp.where(spot, dotted, gram)
-
+    finish()
     for copy in st_list:
         copy.wait_recv()
 
@@ -621,6 +634,19 @@
 
     drains.append(lambda: lax.fori_loop(0, 8, rx_drain, 0))
 
+    bas[0:6, :, 0:ROWS] = bas_own[...]
+    bas[6, :, 0:ROWS] = dir_own[...]
+    lane8 = lax.broadcasted_iota(jnp.int32, (8, 128), 1)
+    sub8 = lax.broadcasted_iota(jnp.int32, (8, 128), 0)
+    gram = jnp.zeros((8, 128), F32)
+    for a in range(7):
+        for b in range(a, 7):
+            dotted = jnp.sum(jnp.sum(bas[a] * bas[b], axis=0, keepdims=True), axis=1, keepdims=True)
+            spot = jnp.logical_and(sub8 == a, lane8 == 64 + b)
+            if a != b:
+                spot = jnp.logical_or(spot, jnp.logical_and(sub8 == b, lane8 == 64 + a))
+            gram = jnp.where(spot, dotted, gram)
+
     def rx_sum(yi):
         cols = slice_of(yi)
         total = py[cols, 0:CUT]
@@ -746,7 +772,8 @@
 
     rows = [jnp.sum(bas[a] * product, axis=0, keepdims=True) for a in range(7)]
     rows.append(jnp.sum(product * product, axis=0, keepdims=True))
-    sums = jnp.concatenate(rows + [gram], axis=0)
+    sums = jnp.concatenate(rows, axis=0)
+    sums = jnp.where(lane8 < 64, sums + pltpu.roll(sums, 64, 1), gram)
 
     def all_sum(stage, value, own, device):
         ar[stage, own] = value
@@ -782,10 +809,11 @@
     sums = all_sum(0, sums, x * 2 + k, lambda i: (z * 8 + i, y))
     sums = all_sum(1, sums, z, lambda i: (i * 8 + x * 2 + k, y))
     sums = all_sum(2, sums, y, lambda i: (ctx, i))
-    inner = jnp.sum(sums[0:8], axis=1, keepdims=True)
+    inner = jnp.sum(jnp.where(lane8 < 64, sums, 0.0), axis=1, keepdims=True)
     coef = jnp.broadcast_to(inner / ENTRIES, (8, 128))
-    coef_row = jnp.sum(jnp.where(jnp.logical_and(sub8 == lane8, sub8 < 7), coef, 0.0), axis=0, keepdims=True)
-    quad = jnp.sum(coef_row * sums[8:16], axis=1, keepdims=True)
+    spots = jnp.logical_and(sub8 == lane8 % 64, sub8 < 7)
+    coef_row = jnp.sum(jnp.where(spots, coef, 0.0), axis=0, keepdims=True)
+    quad = jnp.sum(jnp.where(lane8 < 64, 0.0, coef_row * sums), axis=1, keepdims=True)
     norm = jnp.where(sub8 < 7, coef * (quad - 2.0 * inner), jnp.broadcast_to(inner, (8, 128)))
     squared = jnp.maximum(jnp.sum(norm, axis=0, keepdims=True), 0.0) / ENTRIES
     beta = jnp.sqrt(squared + EPSILON)
@@ -797,6 +825,12 @@
     beta_out[...] = beta[:, 0:1]
 
     finish()
+
+
+def hand_over(coef_in, beta_in, next_in, coef_out, beta_out, next_out):
+    coef_out[...] = coef_in[...]
+    beta_out[...] = beta_in[...]
+    next_out[...] = next_in[...]
 
 
 def body(
@@ -816,10 +850,18 @@
     out, coefficients, beta = pl.pallas_call(
         kernel,
         out_shape=tuple(jax.ShapeDtypeStruct(shape, F32) for shape in ((16, ROWS), (1, 7), (1, 1))),
-        in_specs=[pl.BlockSpec(memory_space=pl.ANY)] + [vmem] * 10,
+        in_specs=[pl.BlockSpec(memory_space=pl.ANY)] * 11,
         out_specs=(vmem,) * 3,
         scratch_shapes=[
             pltpu.VMEM((128, D), BF16),
+            pltpu.VMEM((D // 128, 128), BF16),
+            pltpu.VMEM((128, 128), BF16),
+            pltpu.VMEM((1, 128), jnp.int32),
+            pltpu.VMEM((16, ROWS), BF16),
+            pltpu.VMEM((16, ROWS), F32),
+            pltpu.VMEM((1, 128), F32),
+            pltpu.VMEM((1, 128), F32),
+            pltpu.VMEM((6, 16, ROWS), F32),
             pltpu.VMEM((2, 16, 128), BF16),
             pltpu.VMEM((7, 16, 128), F32),
             pltpu.VMEM((8, 16, 128), BF16),
@@ -845,7 +887,7 @@
             pltpu.VMEM((7, 16, GROUP - CUT), BF16),
             pltpu.VMEM((8, 16, 128), F32),
             pltpu.VMEM((8, 16, 128), F32),
-            pltpu.VMEM((3, 8, 16, 128), F32),
+            pltpu.VMEM((3, 8, 8, 128), F32),
             pltpu.VMEM((2, 128, 128), F32),
             dma((8,)),
             dma((8,)),
@@ -861,7 +903,7 @@
             dma((4, 8)),
             dma((3,)),
             dma((3,)),
-            dma,
+            dma((11,)),
             dma((16,)),
             dma((16,)),
             dma((3, 8)),
@@ -894,6 +936,13 @@
         jnp.asarray(FREQS),
         jnp.swapaxes(stored_basis, 1, 2),
     )
+    coefficients, beta, out = pl.pallas_call(
+        hand_over,
+        out_shape=tuple(jax.ShapeDtypeStruct(shape, F32) for shape in ((1, 7), (1, 1), (16, ROWS))),
+        in_specs=[vmem] * 3,
+        out_specs=(vmem,) * 3,
+        name="hand_over",
+    )(coefficients, beta, out)
     return coefficients.reshape(7), beta.reshape(()), out.T
 
 

time: 88.6 us -> 84.9 us (0.958)
  local copies, waits for them, and re-layouts: 2.43 us -> 0 us
  between operations: 2.41 us -> 0.64 us
    unnamed x2 -> x0, local copies, waits for them, and re-layouts: 2.43 us -> none
    pallas_call x0 -> x1, Pallas kernels: none -> 1.92 us  [body(): pl.pallas_call(hand_over, out_shape=tuple((jax.ShapeDtypeStruct(shape, F3...]
    pallas_call x1, Pallas kernels: 83.5 us -> 82.1 us  [body(): pl.pallas_call(kernel, out_shape=tuple((jax.ShapeDtypeStruct(shape, F32)...]
where the time goes in v4:
time: 84.9 us; the launch traced here: 84.7 us
  Pallas kernels  84.1 us (99%)
    pallas_call x1, Pallas kernels, body(): pl.pallas_call(kernel, out_shape=tuple((jax.ShapeDtypeStruct(shape, F32)...  82.1 us
    pallas_call x1, Pallas kernels, body(): pl.pallas_call(hand_over, out_shape=tuple((jax.ShapeDtypeStruct(shape, F3...  1.92 us

profile of v4, /device:TPU:1, one launch (start us, length us, event | category | flops | bytes accessed | tf_op | source)
XLA Modules:
  0.0 84.7 jit_solution(8016667810391565456)
XLA Ops:
  0.6 82.1 %lanczos_step.1 = (f32[16,84]{1,0:T(8,128)}, f32[1,7]{1,0:T(1,128)}, f32[1,1]{1,0:T(1,128)}) custom-call(bf16[128,5376]{1,0:T(8,128)(2,1)} %bitcast.12, bf16[42,128]{1,0:T(8,128)(2,1)} %bitcast.17, bf16[128,128]{1,0:T(8,128)(2,1)} %bitcast.14, bf16[128,128]{1,0:T(8,128)(2,1)} %bitcast.15, bf16[128,128]{1,0:T(8,128)(2,1)} %bitcast.16, s32[1,128]{1,0:T(1,128)} %seg_in.1, ...), custom_call_target="tpu_custom_call" | custom-call | tf_op jit(solution)/shard_map/lanczos_step/pallas_call | solution.py:850
  82.8 1.9 %hand_over.1 = (f32[1,7]{1,0:T(1,128)}, f32[1,1]{1,0:T(1,128)}, f32[16,84]{1,0:T(8,128)}) custom-call(f32[1,7]{1,0:T(1,128)} %get-tuple-element.9.coef_in, f32[1,1]{1,0:T(1,128)} %get-tuple-element.10.beta_in, f32[16,84]{1,0:T(8,128)} %get-tuple-element.11.next_in), custom_call_target="tpu_custom_call" | custom-call | tf_op jit(solution)/shard_map/hand_over/pallas_call | solution.py:939

commit v5 on v4

--- a/solution.py
+++ b/solution.py
@@ -56,6 +56,11 @@
 def split(a):
     high = a.astype(BF16)
     return high, (a - high.astype(F32)).astype(BF16)
+
+
+def unrolled(start, end, step):
+    for t in range(start, end):
+        step(t, 0)
 
 
 def ring_step(t):
@@ -245,7 +250,7 @@
 
         return 0
 
-    lax.fori_loop(0, 8, g1_send, 0)
+    unrolled(0, 8, g1_send)
 
     def g1_drain(t, _):
         zi = (z + t) % 8
@@ -256,7 +261,7 @@
 
         return 0
 
-    drains.append(lambda: lax.fori_loop(0, 8, g1_drain, 0))
+    drains.append(lambda: unrolled(0, 8, g1_drain))
 
     @pl.when(half == k)
     def _():
@@ -344,7 +349,7 @@
 
         return 0
 
-    lax.fori_loop(0, 8, g1_wait, 0)
+    unrolled(0, 8, g1_wait)
     for xi in range(4):
 
         @pl.when(x == xi)
@@ -384,13 +389,13 @@
         y_copy(y, (y + far_step(t)) % 8, t).start()
         return 0
 
-    lax.fori_loop(0, 7, y_send, 0)
+    unrolled(0, 7, y_send)
 
     def y_drain(t, _):
         y_copy(y, (y + far_step(t)) % 8, t).wait_send()
         return 0
 
-    drains.append(lambda: lax.fori_loop(0, 7, y_drain, 0))
+    drains.append(lambda: unrolled(0, 7, y_drain))
 
     def x_send(yi):
         for t, dx in enumerate((2, 1, 3)):
@@ -411,7 +416,7 @@
         x_send(src)
         return 0
 
-    lax.fori_loop(0, 7, y_forward, 0)
+    unrolled(0, 7, y_forward)
 
     def x_drain(yi, _):
         for t, dx in enumerate((2, 1, 3)):
@@ -420,7 +425,7 @@
             f_copy(parity, xi, yi).wait_send()
         return 0
 
-    drains.append(lambda: lax.fori_loop(0, 8, x_drain, 0))
+    drains.append(lambda: unrolled(0, 8, x_drain))
 
     def x_forward(t, _):
         yi = (y + ring_step(t - 1)) % 8
@@ -430,7 +435,7 @@
             f_copy(parity, xi, yi).start()
         return 0
 
-    lax.fori_loop(0, 8, x_forward, 0)
+    unrolled(0, 8, x_forward)
 
     for copy in qu_far():
         copy.wait_recv()
@@ -455,7 +460,7 @@
             f_copy(1 - parity, xi, yi).wait_recv()
             return 0
 
-        lax.fori_loop(0, 8, f_wait, 0)
+        unrolled(0, 8, f_wait)
         second = second + dot_nt(nb[xi], wb[xi, 1 - parity])
     kl[1 - parity] = second
     mine = pl.ds(pl.multiple_of(k * 128, 128), 128)
@@ -609,30 +614,33 @@
         return rdma(tb.at[:, slice_of(yi)], sy.at[dy], sy_s.at[dy - 1], sy_r.at[dy - 1], at_y(yi))
 
     for dx in range(4):
-        part = dot_nn(cots, nb[(x + dx) % 4])
-        if dx:
-            ta[dx] = part[:, 0:CUT].astype(BF16)
-        else:
-            py[...] = part
-        tb[dx] = part[:, CUT:GROUP].astype(BF16)
+        part = dot_nn(cots, nb[(x + dx) % 4, :, CUT:GROUP])
+        tb[dx] = part.astype(BF16)
+        if dx == 0:
+            py[:, CUT:GROUP] = part
+
+    def sy_send(t, _):
+        sy_copy(far_step(t)).start()
+        return 0
+
+    unrolled(0, 7, sy_send)
+    for dx in (2, 1, 3):
+        ta[dx] = dot_nn(cots, nb[(x + dx) % 4, :, 0:CUT]).astype(BF16)
 
     def rx_send(t, _):
-        dy = far_step(t)
-        sy_copy(dy).start()
         for dx in (2, 1, 3):
-            rx_copy(dx, (y + dy) % 8).start()
-        return 0
-
-    lax.fori_loop(0, 7, rx_send, 0)
-    for dx in (2, 1, 3):
-        rx_copy(dx, y).start()
+            rx_copy(dx, (y + far_step(t)) % 8).start()
+        return 0
+
+    unrolled(0, 8, rx_send)
+    py[:, 0:CUT] = dot_nn(cots, nb[x, :, 0:CUT])
 
     def rx_drain(yi, _):
         for dx in (2, 1, 3):
             rx_copy(dx, yi).wait_send()
         return 0
 
-    drains.append(lambda: lax.fori_loop(0, 8, rx_drain, 0))
+    drains.append(lambda: unrolled(0, 8, rx_drain))
 
     bas[0:6, :, 0:ROWS] = bas_own[...]
     bas[6, :, 0:ROWS] = dir_own[...]
@@ -666,13 +674,13 @@
         ry_copy(dy).start()
         return 0
 
-    lax.fori_loop(0, 7, y_sum, 0)
+    unrolled(0, 7, y_sum)
 
     def sy_wait(t, _):
         sy_copy(ring_step(t)).wait_recv()
         return 0
 
-    lax.fori_loop(0, 7, sy_wait, 0)
+    unrolled(0, 7, sy_wait)
 
     def sx_copy(dx):
         return rdma(sx.at[dx], sx.at[3 + dx], sx_s.at[dx - 1], sx_r.at[dx - 1], at_x((x + dx) % 4))
@@ -691,7 +699,7 @@
         ry_copy(ring_step(t)).wait_recv()
         return 0
 
-    lax.fori_loop(0, 7, ry_wait, 0)
+    unrolled(0, 7, ry_wait)
     for dy in range(1, 8):
         total_a = total_a + ry[dy].astype(F32)
     for dx in (1, 3, 2):
@@ -704,7 +712,7 @@
         sy_copy(t + 1).wait_send()
         return 0
 
-    drains.append(lambda: lax.fori_loop(0, 7, ry_drain, 0))
+    drains.append(lambda: unrolled(0, 7, ry_drain))
 
     def pz_copy(slot, src_z):
         zi = k * 4 + slot // 2
@@ -744,7 +752,7 @@
 
         return 0
 
-    lax.fori_loop(0, 8, pz_send, 0)
+    unrolled(0, 8, pz_send)
 
     def pz_drain(slot, _):
         @pl.when(jnp.logical_not(pz_self(slot)))
@@ -753,7 +761,7 @@
 
         return 0
 
-    drains.append(lambda: lax.fori_loop(0, 8, pz_drain, 0))
+    drains.append(lambda: unrolled(0, 8, pz_drain))
 
     def rz_wait(t, _):
         src = (z + t) % 8
@@ -764,7 +772,7 @@
 
         return 0
 
-    lax.fori_loop(0, 8, rz_wait, 0)
+    unrolled(0, 8, rz_wait)
     product = rz[0]
     for src in range(1, 8):
         product = product + rz[src]
@@ -787,14 +795,14 @@
             copy(own, t, (own + far_step(t)) % 8).start()
             return 0
 
-        lax.fori_loop(0, 7, send, 0)
+        unrolled(0, 7, send)
         finish()
 
         def wait(t, _):
             copy((own + ring_step(t)) % 8, 0, own).wait_recv()
             return 0
 
-        lax.fori_loop(0, 7, wait, 0)
+        unrolled(0, 7, wait)
         total = ar[stage, 0]
         for i in range(1, 8):
             total = total + ar[stage, i]
@@ -803,7 +811,7 @@
             copy(own, t, (own + far_step(t)) % 8).wait_send()
             return 0
 
-        drains.append(lambda: lax.fori_loop(0, 7, drain, 0))
+        drains.append(lambda: unrolled(0, 7, drain))
         return total
 
     sums = all_sum(0, sums, x * 2 + k, lambda i: (z * 8 + i, y))

time: 84.9 us -> 84.2 us (level)
  no operation moved by 1% of the time
where the time goes in v5:
time: 84.2 us; the launch traced here: 84 us
  Pallas kernels  83.4 us (99%)
    pallas_call x1, Pallas kernels, body(): pl.pallas_call(kernel, out_shape=tuple((jax.ShapeDtypeStruct(shape, F32)...  81.5 us
    pallas_call x1, Pallas kernels, body(): pl.pallas_call(hand_over, out_shape=tuple((jax.ShapeDtypeStruct(shape, F3...  1.92 us

profile of v5, /device:TPU:1, one launch (start us, length us, event | category | flops | bytes accessed | tf_op | source)
XLA Modules:
  0.0 84.0 jit_solution(1094287511810475264)
XLA Ops:
  0.6 81.5 %lanczos_step.1 = (f32[16,84]{1,0:T(8,128)}, f32[1,7]{1,0:T(1,128)}, f32[1,1]{1,0:T(1,128)}) custom-call(bf16[128,5376]{1,0:T(8,128)(2,1)} %bitcast.12, bf16[42,128]{1,0:T(8,128)(2,1)} %bitcast.17, bf16[128,128]{1,0:T(8,128)(2,1)} %bitcast.14, bf16[128,128]{1,0:T(8,128)(2,1)} %bitcast.15, bf16[128,128]{1,0:T(8,128)(2,1)} %bitcast.16, s32[1,128]{1,0:T(1,128)} %seg_in.1, ...), custom_call_target="tpu_custom_call" | custom-call | tf_op jit(solution)/shard_map/lanczos_step/pallas_call | solution.py:858
  82.1 1.9 %hand_over.1 = (f32[1,7]{1,0:T(1,128)}, f32[1,1]{1,0:T(1,128)}, f32[16,84]{1,0:T(8,128)}) custom-call(f32[1,7]{1,0:T(1,128)} %get-tuple-element.9.coef_in, f32[1,1]{1,0:T(1,128)} %get-tuple-element.10.beta_in, f32[16,84]{1,0:T(8,128)} %get-tuple-element.11.next_in), custom_call_target="tpu_custom_call" | custom-call | tf_op jit(solution)/shard_map/hand_over/pallas_call | solution.py:947

commit v6 on v5

--- a/solution.py
+++ b/solution.py
@@ -615,7 +615,7 @@
 
     for dx in range(4):
         part = dot_nn(cots, nb[(x + dx) % 4, :, CUT:GROUP])
-        tb[dx] = part.astype(BF16)
+        tb[dx] = part
         if dx == 0:
             py[:, CUT:GROUP] = part
 
@@ -625,7 +625,7 @@
 
     unrolled(0, 7, sy_send)
     for dx in (2, 1, 3):
-        ta[dx] = dot_nn(cots, nb[(x + dx) % 4, :, 0:CUT]).astype(BF16)
+        ta[dx] = dot_nn(cots, nb[(x + dx) % 4, :, 0:CUT])
 
     def rx_send(t, _):
         for dx in (2, 1, 3):
@@ -660,7 +660,7 @@
         total = py[cols, 0:CUT]
         for dx in (1, 3, 2):
             rx_copy(dx, yi).wait_recv()
-            total = total + rx[dx - 1, cols, :].astype(F32)
+            total = total + rx[dx - 1, cols, :]
         return total
 
     def ry_copy(dy):
@@ -670,7 +670,7 @@
     def y_sum(t, _):
         dy = far_step(t)
         yi = (y + dy) % 8
-        ta[0, slice_of(yi), :] = rx_sum(yi).astype(BF16)
+        ta[0, slice_of(yi), :] = rx_sum(yi)
         ry_copy(dy).start()
         return 0
 
@@ -686,11 +686,11 @@
         return rdma(sx.at[dx], sx.at[3 + dx], sx_s.at[dx - 1], sx_r.at[dx - 1], at_x((x + dx) % 4))
 
     for dx in (2, 1, 3, 0):
-        part = tb[dx, slice_of(y), :].astype(F32) if dx else py[slice_of(y), CUT:GROUP]
+        part = tb[dx, slice_of(y), :] if dx else py[slice_of(y), CUT:GROUP]
         for dy in range(1, 8):
-            part = part + sy[dy, dx].astype(F32)
+            part = part + sy[dy, dx]
         if dx:
-            sx[dx] = part.astype(BF16)
+            sx[dx] = part
             sx_copy(dx).start()
             drains.append(sx_copy(dx).wait_send)
     total_a = rx_sum(y)
@@ -701,10 +701,10 @@
 
     unrolled(0, 7, ry_wait)
     for dy in range(1, 8):
-        total_a = total_a + ry[dy].astype(F32)
+        total_a = total_a + ry[dy]
     for dx in (1, 3, 2):
         sx_copy(dx).wait_recv()
-        part = part + sx[3 + dx].astype(F32)
+        part = part + sx[3 + dx]
     total = jnp.concatenate([total_a, part], axis=1)
 
     def ry_drain(t, _):
@@ -886,13 +886,13 @@
             pltpu.VMEM((17, 9, 8, 128), F32),
             pltpu.VMEM((2, 128, 128), BF16),
             pltpu.VMEM((256, 128), F32),
-            pltpu.VMEM((4, 128, CUT), BF16),
-            pltpu.VMEM((4, 128, GROUP - CUT), BF16),
-            pltpu.VMEM((3, 128, CUT), BF16),
+            pltpu.VMEM((4, 128, CUT), F32),
+            pltpu.VMEM((4, 128, GROUP - CUT), F32),
+            pltpu.VMEM((3, 128, CUT), F32),
             pltpu.VMEM((128, GROUP), F32),
-            pltpu.VMEM((8, 16, CUT), BF16),
-            pltpu.VMEM((8, 4, 16, GROUP - CUT), BF16),
-            pltpu.VMEM((7, 16, GROUP - CUT), BF16),
+            pltpu.VMEM((8, 16, CUT), F32),
+            pltpu.VMEM((8, 4, 16, GROUP - CUT), F32),
+            pltpu.VMEM((7, 16, GROUP - CUT), F32),
             pltpu.VMEM((8, 16, 128), F32),
             pltpu.VMEM((8, 16, 128), F32),
             pltpu.VMEM((3, 8, 8, 128), F32),

time: 84.2 us -> 90.9 us (1.080)
  Pallas kernels: 83.4 us -> 89.7 us
    pallas_call x1, Pallas kernels: 81.5 us -> 87.8 us  [body(): pl.pallas_call(kernel, out_shape=tuple((jax.ShapeDtypeStruct(shape, F32)...]
where the time goes in v6:
time: 90.9 us; the launch traced here: 90.3 us
  Pallas kernels  89.7 us (99%)
    pallas_call x1, Pallas kernels, body(): pl.pallas_call(kernel, out_shape=tuple((jax.ShapeDtypeStruct(shape, F32)...  87.8 us
    pallas_call x1, Pallas kernels, body(): pl.pallas_call(hand_over, out_shape=tuple((jax.ShapeDtypeStruct(shape, F3...  1.92 us

profile of v6, /device:TPU:1, one launch (start us, length us, event | category | flops | bytes accessed | tf_op | source)
XLA Modules:
  0.0 90.3 jit_solution(10422853491351323145)
XLA Ops:
  0.6 87.8 %lanczos_step.1 = (f32[16,84]{1,0:T(8,128)}, f32[1,7]{1,0:T(1,128)}, f32[1,1]{1,0:T(1,128)}) custom-call(bf16[128,5376]{1,0:T(8,128)(2,1)} %bitcast.12, bf16[42,128]{1,0:T(8,128)(2,1)} %bitcast.17, bf16[128,128]{1,0:T(8,128)(2,1)} %bitcast.14, bf16[128,128]{1,0:T(8,128)(2,1)} %bitcast.15, bf16[128,128]{1,0:T(8,128)(2,1)} %bitcast.16, s32[1,128]{1,0:T(1,128)} %seg_in.1, ...), custom_call_target="tpu_custom_call" | custom-call | tf_op jit(solution)/shard_map/lanczos_step/pallas_call | solution.py:858
  88.4 1.9 %hand_over.1 = (f32[1,7]{1,0:T(1,128)}, f32[1,1]{1,0:T(1,128)}, f32[16,84]{1,0:T(8,128)}) custom-call(f32[1,7]{1,0:T(1,128)} %get-tuple-element.9.coef_in, f32[1,1]{1,0:T(1,128)} %get-tuple-element.10.beta_in, f32[16,84]{1,0:T(8,128)} %get-tuple-element.11.next_in), custom_call_target="tpu_custom_call" | custom-call | tf_op jit(solution)/shard_map/hand_over/pallas_call | solution.py:947
